TPU v7x, 128 devices: a whole 4x4x4 slice. The times are simulated.
128 devices in a mesh: dp: 16 (over z_hi, x, core), tensor: 8 (over z_lo, y).
Axes of the slice: x: 4, y: 4, z: 4 (z_hi: 2, z_lo: 2; z = z_hi * 2 + z_lo), core: 2. Of those that a mesh axis runs over, the one named last changes fastest.
Arguments:
- hidden: bfloat16 [8192, 13824], P('dp', 'tensor'), may hold values from -6 to 6
- weight: bfloat16 [13824, 3072], P('tensor', 'dp'), may hold values from -0.0546875 to 0.0546875
- momentum: bfloat16 [16, 13824, 3072], P('dp', 'tensor'), may hold values from -6 to 6
- target: bfloat16 [8192, 3072], P('dp', 'tensor'), may hold values from -6 to 6
- freqs: int32 [48, 8], replicated, may hold values from 0 to 63, as said below
Outputs:
- new_momentum: bfloat16 [16, 13824, 3072], P('dp', 'tensor')
- update: float32 [13824, 3072], P('tensor', 'dp')
Inputs may be any that keep to these rules, and one draw needn't show every extreme that they name: `freqs`: the 8 frequencies of a block are distinct; every block holds 0 and 63.
All inputs are finite; a program needn't handle non-finite values.
Results may differ from a plain program's by a relative error of at most 0.017.
Values may be sent and summed in bfloat16 or wider, within the bound.
No kernel may reach another device: no remote copies, remote signals or barrier semaphores. Data moves between devices by JAX's collectives and lax.ppermute only.
A program may use at most 192 MiB of HBM per device.

v0:
```python
import math

import jax
import jax.numpy as jnp
from jax import lax
from jax.sharding import PartitionSpec as P

CL = 64


decay_rate = 0.9


def cosine_table():
    freq_ids = jnp.arange(CL, dtype=jnp.float32)[:, None]
    cell_ids = jnp.arange(CL, dtype=jnp.float32)[None, :]
    scale_row = jnp.where(freq_ids == 0, math.sqrt(1.0 / CL), math.sqrt(2.0 / CL))
    return scale_row * jnp.cos(math.pi * (2.0 * cell_ids + 1.0) * freq_ids / (2.0 * CL))


def per_device(hidden, weight, momentum, target, freqs):
    highest_mode = lax.Precision.HIGHEST
    row_count = hidden.shape[0]
    local_units = hidden.shape[1]
    partial_value = jnp.dot(
        hidden, lax.all_gather(weight, "dp", axis=1, tiled=True), preferred_element_type=jnp.float32
    )
    summed = lax.psum_scatter(partial_value, "tensor", scatter_dimension=1, tiled=True)
    residual = (summed - target.astype(jnp.float32)).astype(jnp.bfloat16)
    gathered = lax.all_gather(residual, "tensor", axis=1, tiled=True)
    factor = 1.0 / math.sqrt(row_count)
    gradient = (
        lax.dot_general(
            hidden, gathered, (((0,), (0,)), ((), ())), preferred_element_type=jnp.float32
        )
        * factor
    )
    primed = decay_rate * momentum[0].astype(jnp.float32) + gradient
    width_all = primed.shape[1]
    block_count = width_all // CL
    grouped = primed.reshape(local_units, block_count, CL)
    onehot = (freqs[:, :, None] == jnp.arange(CL, dtype=jnp.int32)[None, None, :]).astype(
        jnp.float32
    )
    chosen = jnp.einsum("ckv,vj->ckj", onehot, cosine_table(), precision=highest_mode)
    coeffs = jnp.einsum("fcj,ckj->ckf", grouped, chosen, precision=highest_mode)
    kept_part = grouped - jnp.einsum("ckf,ckj->fcj", coeffs, chosen, precision=highest_mode)
    new_state = kept_part.reshape(local_units, width_all).astype(jnp.bfloat16)[None]
    shared = lax.psum_scatter(
        coeffs.astype(jnp.bfloat16), "dp", scatter_dimension=0, tiled=True
    ).astype(jnp.float32)
    own_count = shared.shape[0]
    own_basis = lax.dynamic_slice_in_dim(chosen, lax.axis_index("dp") * own_count, own_count, 0)
    decoded = jnp.einsum("ckf,ckj->fcj", shared, own_basis, precision=highest_mode)
    update = decoded.reshape(local_units, own_count * CL) / lax.axis_size("dp")
    return (new_state, update)


def solution(mesh):
    in_specs = (
        P("dp", "tensor"),
        P("tensor", "dp"),
        P("dp", "tensor", None),
        P("dp", "tensor"),
        P(),
    )
    out_specs = (P("dp", "tensor", None), P("tensor", "dp"))
    return jax.shard_map(
        per_device, mesh=mesh, in_specs=in_specs, out_specs=out_specs, check_vma=False
    )
```

profile of v0, /device:TPU:1, one launch (start us, length us, event | category | flops | bytes accessed | tf_op | source)
XLA Modules:
  0.0 348.2 jit_solution(3769115833184573941)
XLA Ops:
  7.2 0.0 copy-start
  7.2 0.0 all-gather.3.cloned.1.call-start
  7.2 0.7 all-gather.3.cloned.1.call-update
  7.9 0.0 copy-start.2
  7.9 0.0 copy-start.3
  7.9 0.0 reduce-scatter.3.cloned.1.call-start
  8.0 89.8 %all-gather.3.cloned.1.call-done = bf16[1728,3072]{0,1:T(8,128)(2,1)} async-done(((bf16[1728,192]{0,1:T(8,128)(2,1)}), bf16[1728,3072]{0,1:T(8,128)(2,1)}) %all-gather.3.cloned.1.call-update) | async-done | bytes 10616848 | tf_op jit(solution)/shard_map/all_gather | solution.py:26
  97.8 0.0 copy-done
  97.8 10.4 %fusion.18 = f32[512,3072]{1,0:T(8,128)} fusion(bf16[512,1728]{0,1:T(8,128)(2,1)S(1)} %copy-done, bf16[1728,3072]{0,1:T(8,128)(2,1)} %all-gather.3.cloned.1.call-done), kind=kOutput, calls=%fused_computation.26 | convolution fusion | flops 5435817984 | bytes 18677760 | tf_op jit(solution)/shard_map/dot_general | solution.py:25
  108.2 0.0 reduce-scatter.3.cloned.1.call-update
  108.2 0.0 all-gather.5.cloned.1.call-start
  108.3 70.3 %reduce-scatter.3.cloned.1.call-done = f32[512,384]{1,0:T(8,128)} async-done(((f32[512,3072]{1,0:T(8,128)}), f32[512,384]{1,0:T(8,128)}) %reduce-scatter.3.cloned.1.call-update) | async-done | bytes 786448 | tf_op jit(solution)/shard_map/reduce_scatter | solution.py:28
  178.6 0.0 copy-done.2
  178.6 1.9 subtract_convert_fusion
  180.6 0.0 all-gather.5.cloned.1.call-update
  180.6 0.0 reduce-scatter.5.cloned.1.call-start
  180.6 0.0 copy-done.3
  180.7 0.4 fusion.1
  181.0 40.1 %all-gather.5.cloned.1.call-done = bf16[512,3072]{1,0:T(8,128)(2,1)} async-done(((bf16[512,384]{1,0:T(8,128)(2,1)}), bf16[512,3072]{1,0:T(8,128)(2,1)}) %all-gather.5.cloned.1.call-update) | async-done | bytes 3145744 | tf_op jit(solution)/shard_map/all_gather | solution.py:30
  221.1 14.0 %bitcast_add_fusion = f32[1728,3072]{1,0:T(8,128)} fusion(bf16[1,1728,3072]{2,1,0:T(8,128)(2,1)} %param.7, bf16[512,1728]{0,1:T(8,128)(2,1)S(1)} %copy-done, bf16[512,3072]{1,0:T(8,128)(2,1)} %all-gather.5.cloned.1.call-done), kind=kOutput, calls=%fused_computation.2 | convolution fusion | flops 5457051648 | bytes 36765696 | tf_op jit(solution)/shard_map/dot_general | solution.py:33
  235.1 21.4 %copy.13 = f32[1728,3072]{0,1:T(8,128)} copy(f32[1728,3072]{1,0:T(8,128)} %bitcast_add_fusion) | data formatting | bytes 42467328 | tf_op jit(solution)/shard_map/add | solution.py:38
  256.5 14.6 %fusion.17 = (bf16[48,8,1728]{2,1,0:T(8,128)(2,1)}, f32[48,8,1728]{2,1,0:T(8,128)}) fusion(f32[1728,48,64]{0,2,1:T(8,128)} %bitcast.23, f32[48,8,64]{2,0,1:T(8,128)S(1)} %fusion.1), kind=kOutput, calls=%fused_computation.25 | convolution fusion | flops 510271488 | bytes 25313280 | tf_op jit(solution)/shard_map/fcj,ckj->ckf/dot_general | solution.py:46
  271.2 0.0 reduce-scatter.5.cloned.1.call-update
  271.2 23.5 %fusion = bf16[1728,48,64]{0,2,1:T(8,128)(2,1)} fusion(f32[1728,48,64]{0,2,1:T(8,128)} %bitcast.24, f32[48,8,1728]{2,1,0:T(8,128)} %get-tuple-element.7, f32[48,8,64]{2,0,1:T(8,128)S(1)} %fusion.1), kind=kOutput, calls=%fused_computation.1 | convolution fusion | flops 520224768 | bytes 34603008 | tf_op jit(solution)/shard_map/ckf,ckj->fcj/dot_general | solution.py:47
  294.7 0.0 copy-start.1
  294.7 14.6 %copy.17 = bf16[1,1728,3072]{2,1,0:T(8,128)(2,1)} copy(bf16[1,1728,3072]{1,2,0:T(8,128)(2,1)} %bitcast.25) | data formatting | bytes 21233664
  309.3 29.7 %reduce-scatter.5.cloned.1.call-done = bf16[3,8,1728]{2,1,0:T(8,128)(2,1)} async-done(((bf16[48,8,1728]{2,1,0:T(8,128)(2,1)}), bf16[3,8,1728]{2,1,0:T(8,128)(2,1)}) %reduce-scatter.5.cloned.1.call-update) | async-done | bytes 82960 | tf_op jit(solution)/shard_map/reduce_scatter | solution.py:49
  339.0 2.7 convolution_multiply_fusion
  341.7 0.0 copy-done.1
  (2 shorter events, 0.0 us)
Async XLA Ops:
  7.2 90.7 %copy-start = (bf16[512,1728]{0,1:T(8,128)(2,1)S(1)}, bf16[512,1728]{0,1:T(8,128)(2,1)}, u32[]{:S(2)}) copy-start(bf16[512,1728]{0,1:T(8,128)(2,1)} %param.5) | copy-start | bytes 5308420
  7.2 90.6 %all-gather.3.cloned.1.call-start = ((), (), s32[]{:S(2)}) async-start(), calls=%async_computation.2 | async-start | bytes 11698176 | tf_op jit(solution)/shard_map/all_gather | solution.py:26
  7.9 170.7 %copy-start.2 = (bf16[512,384]{1,0:T(8,128)(2,1)S(1)}, bf16[512,384]{1,0:T(8,128)(2,1)}, u32[]{:S(2)}) copy-start(bf16[512,384]{1,0:T(8,128)(2,1)} %param.8) | copy-start | bytes 1179652
  7.9 172.7 %copy-start.3 = (s32[48,8]{0,1:T(8,128)S(1)}, s32[48,8]{0,1:T(8,128)}, u32[]{:S(2)}) copy-start(s32[48,8]{0,1:T(8,128)} %param.9) | copy-start | bytes 4612
  7.9 170.7 %reduce-scatter.3.cloned.1.call-start = ((), (), s32[]{:S(2)}) async-start(), calls=%async_computation.3 | async-start | bytes 7077888 | tf_op jit(solution)/shard_map/reduce_scatter | solution.py:28
  108.2 112.9 %all-gather.5.cloned.1.call-start = ((), (), s32[]{:S(2)}) async-start(), calls=%async_computation.4 | async-start | bytes 3538944 | tf_op jit(solution)/shard_map/all_gather | solution.py:30
  180.6 158.4 %reduce-scatter.5.cloned.1.call-start = ((), (), s32[]{:S(2)}) async-start(), calls=%async_computation.5 | async-start | bytes 1462272 | tf_op jit(solution)/shard_map/reduce_scatter | solution.py:49
  294.7 47.0 %copy-start.1 = (bf16[512,1728]{0,1:T(8,128)(2,1)S(1)}, bf16[512,1728]{0,1:T(8,128)(2,1)}, u32[]{:S(2)}) copy-start(bf16[512,1728]{0,1:T(8,128)(2,1)} %param.5) | copy-start | bytes 5308420
Sparse Core Ops, SparseCore 0:
  10.4 87.3 all-gather.2
  108.3 70.2 reduce-scatter.2
  180.8 40.2 all-gather.4
  271.3 67.6 reduce-scatter.4
where the time goes:
time: 350 us; the launch traced here: 348 us
  waiting for transfers between devices  231 us (66%)
  matrix products  65.6 us (19%)
  local copies, waits for them, and re-layouts  36.1 us (10%)
  between operations  13.8 us (4%)
    all_gather x1, waiting for transfers between devices, per_device(): lax.all_gather(weight, 'dp', axis=1, tiled=True)  89.8 us
    reduce_scatter x1, waiting for transfers between devices, per_device(): lax.psum_scatter(partial_value, 'tensor', scatter_dimension=1, tiled=True)  70.3 us
    all_gather x1, waiting for transfers between devices, per_device(): gathered = lax.all_gather(residual, 'tensor', axis=1, tiled=True)  40.1 us
    reduce_scatter x1, waiting for transfers between devices, per_device(): lax.psum_scatter(coeffs.astype(jnp.bfloat16), 'dp', scatter_dimension=0,...  29.7 us
    dot_general x1, matrix products, per_device(): jnp.einsum('ckf,ckj->fcj', coeffs, chosen, precision=highest_mode)  23.5 us
    add x1, local copies, waits for them, and re-layouts, per_device(): primed = decay_rate * momentum[0].astype(jnp.float32) + gradient  21.4 us
    unnamed x9, local copies, waits for them, and re-layouts  14.6 us
    dot_general x1, matrix products, per_device(): coeffs = jnp.einsum('fcj,ckj->ckf', grouped, chosen, precision=highest_mode)  14.6 us
  transfers between devices with their start and end apart: 4, of which 4 were waited for; matrix products, arithmetic and copies ran while one was open for 11% of the time, Pallas kernels for 0%

commit v1 on v0

v1 whole, which is shorter than its diff:
```python
import functools
import math

import jax
import jax.numpy as jnp
from jax import lax
from jax.experimental import pallas as pl
from jax.experimental.pallas import tpu as pltpu
from jax.sharding import Mesh, PartitionSpec as P
import numpy as np

CL = 64
DECAY = 0.9
AXES = ("zh", "x", "c", "zl", "y")
DP = ("zh", "x", "c")
TENSOR = ("zl", "y")
CHUNKS = (((0, 0), (1, 0), (0, 1), (0, 3), (0, 2), (1, 1), (1, 3), (1, 2)),)


def cosine_table():
    freq_ids = jnp.arange(CL, dtype=jnp.float32)[:, None]
    cell_ids = jnp.arange(CL, dtype=jnp.float32)[None, :]
    scale_row = jnp.where(freq_ids == 0, math.sqrt(1.0 / CL), math.sqrt(2.0 / CL))
    return scale_row * jnp.cos(math.pi * (2.0 * cell_ids + 1.0) * freq_ids / (2.0 * CL))


def shift(sizes, **by):
    step = [by.get(a, 0) for a in AXES]
    pairs = []
    for at in np.ndindex(*sizes):
        to = [(a + s) % n for a, s, n in zip(at, step, sizes)]
        pairs.append((int(np.ravel_multi_index(at, sizes)), int(np.ravel_multi_index(to, sizes))))
    return pairs


def output_kernel(n, info, ht_ref, target_ref, *refs):
    out_ref = refs[-1]
    core = info[0]
    half = refs[0].shape[0]
    for u in range(n):
        for which in range(2):
            w_ref = refs[2 * u + which]
            slot = core if which == 0 else 1 - core
            value = jnp.dot(w_ref[...], ht_ref[...], preferred_element_type=jnp.float32)
            rows = pl.ds(pl.multiple_of((2 * u + slot) * half, half), half)
            out_ref[rows, :] = value.astype(jnp.bfloat16)

        @pl.when(info[1 + u] != 0)
        def _():
            rows = pl.ds(2 * u * half, 2 * half)
            goal = target_ref[...].astype(jnp.float32).T
            out_ref[rows, :] = (out_ref[rows, :].astype(jnp.float32) - goal).astype(jnp.bfloat16)


def partial_output(info, ht, target, blocks):
    n = len(blocks) // 2
    half, depth = blocks[0].shape
    tokens = ht.shape[1]
    vmem = pl.BlockSpec(memory_space=pltpu.VMEM)
    return pl.pallas_call(
        functools.partial(output_kernel, n),
        out_shape=jax.ShapeDtypeStruct((2 * n * half, tokens), jnp.bfloat16),
        in_specs=[pl.BlockSpec(memory_space=pltpu.SMEM)] + [vmem] * (2 + len(blocks)),
        out_specs=vmem,
        compiler_params=pltpu.CompilerParams(vmem_limit_bytes=48 * 2**20),
        cost_estimate=pl.CostEstimate(
            flops=4 * n * half * depth * tokens,
            bytes_accessed=2 * (2 * n * half * (depth + tokens) + depth * tokens),
            transcendentals=0,
        ),
    )(info, ht, target, *blocks)


def step_kernel(factor, first, info, ht_ref, rt_ref, m_ref, keep_ref, code_ref, *refs):
    new_ref, mine_ref, other_ref = refs[-3:]
    rows = m_ref.shape[0]
    width = m_ref.shape[1]
    mine = mine_ref.shape[0]
    rt = rt_ref[...]
    keep = keep_ref[0]
    code = code_ref[0]
    for start in range(0, rows, 512):
        size = min(512, rows - start)
        f = pl.ds(start, size)
        grad = lax.dot_general(
            ht_ref[f, :], rt, (((1,), (1,)), ((), ())), preferred_element_type=jnp.float32
        )
        primed = DECAY * m_ref[f, :].astype(jnp.float32) + grad * factor
        low = primed.astype(jnp.bfloat16)
        for a in range(0, width, 256):
            b = min(a + 256, width)
            gone = jnp.dot(low[:, a:b], keep[a:b, a:b], preferred_element_type=jnp.float32)
            new_ref[f, a:b] = (primed[:, a:b] - gone).astype(jnp.bfloat16)
        coeffs = lax.dot_general(
            code, low, (((1,), (1,)), ((), ())), preferred_element_type=jnp.float32
        ).astype(jnp.bfloat16)
        mine_ref[:, f] = coeffs[:mine]
        other_ref[:, f] = coeffs[mine:]


def momentum_step(chips, ht, rt, momentum, keep, code, state, factor):
    n = chips.shape[0]
    rows, width_all = momentum.shape
    tokens = ht.shape[1]
    width = rt.shape[0] // n
    kept = code.shape[1]
    mine = kept // 2
    in_specs = [
        pl.BlockSpec((rows, tokens), lambda u, c: (0, 0)),
        pl.BlockSpec((width, tokens), lambda u, c: (u, 0)),
        pl.BlockSpec((rows, width), lambda u, c: (0, c[u])),
        pl.BlockSpec((1, width, width), lambda u, c: (c[u], 0, 0)),
        pl.BlockSpec((1, kept, width), lambda u, c: (c[u], 0, 0)),
    ]
    args = [ht, rt, momentum, keep, code]
    alias = {}
    if state is not None:
        in_specs.append(pl.BlockSpec(memory_space=pl.ANY))
        args.append(state)
        alias = {6: 0}
    return pl.pallas_call(
        functools.partial(step_kernel, factor, state is None),
        out_shape=(
            jax.ShapeDtypeStruct((rows, width_all), jnp.bfloat16),
            jax.ShapeDtypeStruct((n, mine, rows), jnp.bfloat16),
            jax.ShapeDtypeStruct((n, mine, rows), jnp.bfloat16),
        ),
        grid_spec=pltpu.PrefetchScalarGridSpec(
            num_scalar_prefetch=1,
            grid=(n,),
            in_specs=in_specs,
            out_specs=(
                pl.BlockSpec((rows, width), lambda u, c: (0, c[u])),
                pl.BlockSpec((None, mine, rows), lambda u, c: (u, 0, 0)),
                pl.BlockSpec((None, mine, rows), lambda u, c: (u, 0, 0)),
            ),
        ),
        input_output_aliases=alias,
        compiler_params=pltpu.CompilerParams(
            vmem_limit_bytes=48 * 2**20, dimension_semantics=("arbitrary",)
        ),
        cost_estimate=pl.CostEstimate(
            flops=2 * n * rows * width * (tokens + 256 + kept),
            bytes_accessed=2 * (2 * n * rows * width + rows * tokens),
            transcendentals=0,
        ),
    )(chips, *args)


def tables(freqs, core, n_chips):
    onehot = (freqs[:, :, None] == jnp.arange(CL, dtype=jnp.int32)[None, None, :]).astype(jnp.float32)
    chosen = jnp.einsum("ckv,vj->ckj", onehot, cosine_table(), precision=lax.Precision.HIGHEST)
    blocks, kept, _ = chosen.shape
    per = blocks // n_chips
    same = jnp.eye(per, dtype=jnp.float32)
    proj = jnp.einsum("ckj,ckl->cjl", chosen, chosen, precision=lax.Precision.HIGHEST)
    proj = proj.reshape(n_chips, per, CL, 1, CL) * same[None, :, None, :, None]
    keep = proj.reshape(n_chips, per * CL, per * CL).astype(jnp.bfloat16)
    code = chosen.reshape(n_chips, per, kept, 1, CL) * same[None, :, None, :, None]
    code = code.reshape(n_chips, 2, per * kept // 2, per * CL)
    code = jnp.where(core == 0, code, code[:, ::-1]).reshape(n_chips, per * kept, per * CL)
    return chosen, keep, code.astype(jnp.bfloat16)


def per_device(sizes, hidden, weight, momentum, target, freqs):
    send = lambda v, **by: lax.ppermute(v, AXES, shift(sizes, **by))
    zh, x, c = (lax.axis_index(a) for a in DP)
    n_zh, n_x = sizes[0], sizes[1]
    n_tensor = sizes[3] * sizes[4]
    shard = lax.axis_index(TENSOR)
    chip_at = lambda s: ((zh + s[0]) % n_zh) * n_x + (x + s[1]) % n_x

    ht = hidden.T
    own = weight.T
    factor = 1.0 / math.sqrt(hidden.shape[0])

    blocks = {(0, 0): own}
    blocks[1, 0] = send(own, zh=1)
    blocks[0, 1] = send(own, x=-1)
    blocks[0, 3] = send(own, x=1)
    blocks[0, 2] = send(own, x=2)
    blocks[1, 1] = send(blocks[1, 0], x=-1)
    blocks[1, 3] = send(blocks[1, 0], x=1)
    blocks[1, 2] = send(blocks[0, 2], zh=1)
    swapped = {s: send(b, c=1) for s, b in blocks.items()}

    chosen, keep, code = tables(freqs, c, n_zh * n_x)

    state = None
    parts = []
    for chunk in CHUNKS:
        n = len(chunk)
        chips = jnp.stack([chip_at(s) for s in chunk]).astype(jnp.int32)
        info = jnp.concatenate([c[None].astype(jnp.int32), (chips == shard).astype(jnp.int32)])
        pairs = [b for s in chunk for b in (blocks[s], swapped[s])]
        partial = partial_output(info, ht, target, pairs)
        split = partial.reshape(n_tensor, partial.shape[0] // n_tensor, partial.shape[1])
        received = lax.all_to_all(split, TENSOR, 0, 0)
        residual = jnp.sum(received.astype(jnp.float32), axis=0).astype(jnp.bfloat16)
        gathered = lax.all_gather(residual, TENSOR, axis=0, tiled=True)
        state, mine, other = momentum_step(chips, ht, gathered, momentum[0], keep, code, state, factor)
        pair = (mine.astype(jnp.float32) + send(other, c=1).astype(jnp.float32)).astype(jnp.bfloat16)
        for u, s in enumerate(chunk):
            parts.append(pair[u] if s == (0, 0) else send(pair[u], zh=s[0], x=s[1]))

    total = sum(p.astype(jnp.float32) for p in parts)
    per = chosen.shape[0] // (n_zh * n_x * sizes[2])
    own_basis = lax.dynamic_slice_in_dim(chosen, lax.axis_index(DP) * per, per, 0)
    decoded = jnp.einsum(
        "ckf,ckj->cjf",
        total.reshape(per, total.shape[0] // per, total.shape[1]),
        own_basis * (1.0 / (n_zh * n_x * sizes[2])),
        precision=lax.Precision.HIGHEST,
    )
    return state[None], decoded.reshape(per * CL, -1).T


def solution(mesh):
    sizes = (2, 4, 2, 2, 4)
    fine = Mesh(mesh.devices.reshape(sizes), AXES)
    in_specs = (P(DP, TENSOR), P(TENSOR, DP), P(DP, TENSOR, None), P(DP, TENSOR), P())
    out_specs = (P(DP, TENSOR, None), P(TENSOR, DP))
    return jax.shard_map(
        functools.partial(per_device, sizes),
        mesh=fine,
        in_specs=in_specs,
        out_specs=out_specs,
        check_vma=False,
    )
```

time: 350 us -> 227 us (0.65)
  waiting for transfers between devices: 231 us -> 50.2 us
  matrix products: 65.6 us -> 5.34 us
  starting transfers between devices: 0.16 us -> 49.8 us
  blocking collectives: 0 us -> 42.3 us
  Pallas kernels: 0 us -> 32.1 us
  local copies, waits for them, and re-layouts: 36.1 us -> 24.8 us
  other arithmetic: 1.96 us -> 6.43 us
    all_gather x2 -> x1, waiting for transfers between devices: 130 us -> 16.3 us  [per_device(): gathered = lax.all_gather(residual, TENSOR, axis=0, tiled=True)]
    reduce_scatter x2 -> x0, waiting for transfers between devices: 100 us -> none  [the longest x1 70.3 us: per_device(): lax.psum_scatter(partial_value, 'tensor', scatter_dimension=1, tiled=True)]
    dot_general x6 -> x3, matrix products: 65.6 us -> 5.34 us  [the longest x1 2.63 us: tables(): jnp.einsum('ckj,ckl->cjl', chosen, chosen, precision=lax.Precision.HIGHEST)]
    ppermute x0 -> x23, starting transfers between devices: none -> 49.7 us  [per_device(): send = lambda v, **by: lax.ppermute(v, AXES, shift(sizes, **by))]
    all_to_all x0 -> x1, blocking collectives: none -> 42.3 us  [per_device(): received = lax.all_to_all(split, TENSOR, 0, 0)]
    ppermute x0 -> x23, waiting for transfers between devices: none -> 33.9 us  [per_device(): send = lambda v, **by: lax.ppermute(v, AXES, shift(sizes, **by))]
    pallas_call x0 -> x2, Pallas kernels: none -> 32.1 us  [the longest x1 19.9 us: momentum_step(): pl.pallas_call(functools.partial(step_kernel, factor, state is None), out...]
    add x1 -> x0, local copies, waits for them, and re-layouts: 21.4 us -> none  [per_device(): primed = decay_rate * momentum[0].astype(jnp.float32) + gradient]
  transfers between devices with their start and end apart: 4 -> 24, of which waited for: 4 -> 13; matrix products, arithmetic and copies ran while one was open for 11% -> 10% of each run, Pallas kernels for 0% -> 0%
where the time goes in v1:
time: 227 us; the launch traced here: 225 us
  waiting for transfers between devices  50.2 us (22%)
  starting transfers between devices  49.8 us (22%)
  blocking collectives  42.3 us (19%)
  Pallas kernels  32.1 us (14%)
  local copies, waits for them, and re-layouts  24.8 us (11%)
  between operations  14.2 us (6%)
  other arithmetic  6.43 us (3%)
  matrix products  5.34 us (2%)
    ppermute x23, starting transfers between devices, per_device(): send = lambda v, **by: lax.ppermute(v, AXES, shift(sizes, **by))  49.7 us
    all_to_all x1, blocking collectives, per_device(): received = lax.all_to_all(split, TENSOR, 0, 0)  42.3 us
    ppermute x23, waiting for transfers between devices, per_device(): send = lambda v, **by: lax.ppermute(v, AXES, shift(sizes, **by))  33.9 us
    pallas_call x1, Pallas kernels, momentum_step(): pl.pallas_call(functools.partial(step_kernel, factor, state is None), out...  19.9 us
    mul x4, local copies, waits for them, and re-layouts, tables(): proj = proj.reshape(n_chips, per, CL, 1, CL) * same[None, :, None, :, None]  16.4 us
    all_gather x1, waiting for transfers between devices, per_device(): gathered = lax.all_gather(residual, TENSOR, axis=0, tiled=True)  16.3 us
    pallas_call x1, Pallas kernels, partial_output(): pl.pallas_call(functools.partial(output_kernel, n), out_shape=jax.ShapeDt...  12.2 us
    unnamed x16, local copies, waits for them, and re-layouts  7.46 us
  transfers between devices with their start and end apart: 24, of which 13 were waited for; matrix products, arithmetic and copies ran while one was open for 10% of the time, Pallas kernels for 0%

profile of v1, /device:TPU:1, one launch (start us, length us, event | category | flops | bytes accessed | tf_op | source)
XLA Modules:
  0.0 225.1 jit_solution(997250188342871795)
XLA Ops:
  7.2 0.0 all-gather.2.cloned.1.call-start
  7.2 4.5 %collective-permute-start.1 = (bf16[192,1728]{1,0:T(8,128)(2,1)}, bf16[192,1728]{1,0:T(8,128)(2,1)S(1)}, u32[]{:S(2)}, u32[]{:S(2)}) collective-permute-start(bf16[192,1728]{1,0:T(8,128)(2,1)} %bitcast.49), channel_id=1, source_target_pairs={{0,64},{1,65},{2,66},{3,67},{4,68},{5,69},{6,70},{7,71},{8,72},{9,... | collective-permute-start | bytes 1990664 | tf_op jit(solution)/shard_map/ppermute | solution.py:166
  11.7 2.5 %collective-permute-start.3 = (bf16[192,1728]{1,0:T(8,128)(2,1)}, bf16[192,1728]{1,0:T(8,128)(2,1)S(1)}, u32[]{:S(2)}, u32[]{:S(2)}) collective-permute-start(bf16[192,1728]{1,0:T(8,128)(2,1)} %bitcast.50), channel_id=1, source_target_pairs={{0,48},{1,49},{2,50},{3,51},{4,52},{5,53},{6,54},{7,55},{8,56},{9,... | collective-permute-start | bytes 1990664 | tf_op jit(solution)/shard_map/ppermute | solution.py:166
  14.2 1.2 collective-permute-start
  15.4 1.7 collective-permute-start.7
  17.2 9.9 %collective-permute-done.1.refs_2_ = bf16[192,1728]{1,0:T(8,128)(2,1)S(1)} collective-permute-done((bf16[192,1728]{1,0:T(8,128)(2,1)}, bf16[192,1728]{1,0:T(8,128)(2,1)S(1)}, u32[]{:S(2)}, u32[]{:S(2)}) %collective-permute-start.1) | collective-permute-done | bytes 663584 | tf_op jit(solution)/shard_map/ppermute | solution.py:166
  27.1 1.2 collective-permute-start.2
  28.3 0.8 collective-permute-done.3.refs_4_
  29.1 15.8 %collective-permute-start.4 = (bf16[192,1728]{1,0:T(8,128)(2,1)S(1)}, bf16[192,1728]{1,0:T(8,128)(2,1)S(1)}, u32[]{:S(2)}, u32[]{:S(2)}) collective-permute-start(bf16[192,1728]{1,0:T(8,128)(2,1)S(1)} %collective-permute-done.3.refs_4_), channel_id=1, source_target_pairs={{0,8},{1,9},{2,10},{3,11},{4,12},{5,13},{6,14},{7,15},{8,0},{9,1},... | collective-permute-start | bytes 1990664 | tf_op jit(solution)/shard_map/ppermute | solution.py:166
  44.9 3.3 %collective-permute-start.9 = (bf16[192,1728]{1,0:T(8,128)(2,1)S(1)}, bf16[192,1728]{1,0:T(8,128)(2,1)}, u32[]{:S(2)}, u32[]{:S(2)}) collective-permute-start(bf16[192,1728]{1,0:T(8,128)(2,1)S(1)} %collective-permute-done.1.refs_2_), channel_id=1, source_target_pairs={{0,48},{1,49},{2,50},{3,51},{4,52},{5,53},{6,54},{7,55},{8,56},{9,... | collective-permute-start | bytes 1990664 | tf_op jit(solution)/shard_map/ppermute | solution.py:166
  48.2 0.4 collective-permute-done.5.refs_6_
  48.7 0.0 copy-start.2
  48.7 0.8 copy-done.2
  49.5 0.9 collective-permute-start.8
  50.4 0.0 collective-permute-done.4.refs_5_
  50.4 0.8 copy-done.4
  51.2 0.0 collective-permute-start.6
  51.2 11.8 %collective-permute-done.9.refs_10_ = bf16[192,1728]{1,0:T(8,128)(2,1)} collective-permute-done((bf16[192,1728]{1,0:T(8,128)(2,1)S(1)}, bf16[192,1728]{1,0:T(8,128)(2,1)}, u32[]{:S(2)}, u32[]{:S(2)}) %collective-permute-start.9) | collective-permute-done | bytes 663584 | tf_op jit(solution)/shard_map/ppermute | solution.py:166
  63.1 0.8 collective-permute-start.10
  63.9 2.3 %collective-permute-done.11.refs_12_ = bf16[192,1728]{1,0:T(8,128)(2,1)} collective-permute-done((bf16[192,1728]{1,0:T(8,128)(2,1)S(1)}, bf16[192,1728]{1,0:T(8,128)(2,1)}, u32[]{:S(2)}, u32[]{:S(2)}) %collective-permute-start.11) | collective-permute-done | bytes 663584 | tf_op jit(solution)/shard_map/ppermute | solution.py:166
  66.2 1.7 collective-permute-start.12
  67.8 0.5 collective-permute-start.14
  68.3 0.1 stack.35.info
  68.4 0.1 pad_add_fusion.info
  68.5 1.4 collective-permute-done.12.refs_13_
  69.9 1.0 collective-permute-done.14.refs_15_
  70.9 1.1 copy-done.1
  72.0 1.1 copy-done.3
  73.1 1.1 copy-done.5
  74.2 1.0 copy-done.6
  75.2 12.2 %shard_map.68 = bf16[3072,512]{1,0:T(8,128)(2,1)} custom-call(s32[9]{0:T(128)S(1)} %pad_add_fusion.info, bf16[1728,512]{1,0:T(8,128)(2,1)} %bitcast.47, bf16[512,384]{1,0:T(8,128)(2,1)S(1)} %copy-done.6, bf16[192,1728]{1,0:T(8,128)(2,1)S(1)} %bitcast.54, bf16[192,1728]{1,0:T(8,128)(2,1)S(1)} %collective-permute-done.refs_1_, ...), custom_call_target="tpu_custom_call" | custom-call | flops 5435817984 | bytes 15532032 | tf_op jit(solution)/shard_map/pallas_call | solution.py:60
  87.4 42.3 %all_to_all.5 = bf16[8,384,512]{2,1,0:T(8,128)(2,1)} all-to-all(bf16[8,384,512]{2,1,0:T(8,128)(2,1)} %bitcast.56), channel_id=1, replica_groups=mesh['zh'=2,'x'=4,'c'=2,'zl'=2,'y'=4] {'zl','y'}, dimensions={0} | all-to-all | bytes 6291456 | tf_op jit(solution)/shard_map/all_to_all | solution.py:198
  129.7 3.2 %reduce_sum.12 = bf16[384,512]{1,0:T(8,128)(2,1)} reduce(bf16[8,384,512]{2,1,0:T(8,128)(2,1)} %all_to_all.5, bf16[]{:T(256)} %constant.95.clone.1), dimensions={0}, to_apply=%region_0.1 | reduce | flops 1376256 | bytes 3538946 | tf_op jit(solution)/shard_map/reduce_sum | solution.py:199
  132.9 0.0 all-gather.2.cloned.1.call-update
  132.9 0.4 fusion.1
  133.3 0.1 copy.15
  133.4 2.6 %fusion.35 = f32[48,64,64]{2,1,0:T(8,128)S(1)} fusion(f32[48,8,64]{2,0,1:T(8,128)S(1)} %fusion.1), kind=kOutput, calls=%fused_computation.53 | convolution fusion | flops 18874368 | bytes 884736 | tf_op jit(solution)/shard_map/ckj,ckl->cjl/dot_general | solution.py:156
  136.0 5.5 %mul.130 = f32[8,6,64,6,64]{4,3,2,1,0:T(8,128)} broadcast(f32[8,6,64,64]{3,2,1,0:T(8,128)S(1)} %bitcast.55), dimensions={0,1,2,4} | broadcast | bytes 5505024 | tf_op jit(solution)/shard_map/mul | solution.py:157
  141.5 10.4 %mul.131 = f32[8,384,384]{2,1,0:T(8,128)} reshape(f32[8,6,64,6,64]{4,3,2,1,0:T(8,128)} %mul.130) | data formatting | bytes 9437184 | tf_op jit(solution)/shard_map/mul | solution.py:157
  151.9 0.2 mul.132
  152.0 0.4 mul.133
  152.4 0.2 mul.137
  152.6 0.4 mul.138
  153.0 0.1 mul.139
  153.1 0.1 mul.140
  153.2 0.1 fusion
  153.3 2.9 %multiply_convert_fusion.keep_ref = bf16[8,384,384]{2,1,0:T(8,128)(2,1)S(1)} fusion(f32[8,384,384]{2,1,0:T(8,128)} %mul.131, f32[384,384]{1,0:T(8,128)S(1)} %mul.133), kind=kLoop, calls=%fused_computation | loop fusion | flops 2359296 | bytes 7667712 | tf_op jit(solution)/shard_map/convert_element_type | solution.py:158
  156.2 16.3 %all-gather.2.cloned.1.call-done.rt_ref = bf16[3072,512]{1,0:T(8,128)(2,1)} async-done(((bf16[384,512]{1,0:T(8,128)(2,1)}), bf16[3072,512]{1,0:T(8,128)(2,1)}) %all-gather.2.cloned.1.call-update) | async-done | bytes 3145744 | tf_op jit(solution)/shard_map/all_gather | solution.py:200
  172.5 1.5 copy-done
  173.9 19.9 %shard_map.69 = (bf16[1728,3072]{1,0:T(8,128)(2,1)}, bf16[8,24,1728]{2,1,0:T(8,128)(2,1)S(1)}, bf16[8,24,1728]{2,1,0:T(8,128)(2,1)S(1)}) custom-call(s32[8]{0:T(128)S(1)} %stack.35.info, bf16[1728,512]{1,0:T(8,128)(2,1)S(1)} %bitcast.48, bf16[3072,512]{1,0:T(8,128)(2,1)} %all-gather.2.cloned.1.call-done.rt_ref, bf16[1728,3072]{1,0:T(8,128)(2,1)} %bitcast.59, ...), custom_call_target="tpu_custom_call" | custom-call | flops 8663334912 | bytes 23003136 | tf_op jit(solution)/shard_map/pallas_call | solution.py:121
  193.9 3.3 %collective-permute-start.15 = (bf16[8,24,1728]{2,1,0:T(8,128)(2,1)S(1)}, bf16[8,24,1728]{2,1,0:T(8,128)(2,1)S(1)}, u32[]{:S(2)}, u32[]{:S(2)}) collective-permute-start(bf16[8,24,1728]{2,1,0:T(8,128)(2,1)S(1)} %get-tuple-element.7), channel_id=1, source_target_pairs={{0,8},{1,9},{2,10},{3,11},{4,12},{5,13},{6,14},{7,15},{8,0},{9,1},... | collective-permute-start | bytes 1990664 | tf_op jit(solution)/shard_map/ppermute | solution.py:166
  197.2 1.8 collective-permute-done.15
  198.9 0.2 add_convert_fusion
  199.2 5.1 %collective-permute-start.22 = (bf16[24,1728]{1,0:T(8,128)(2,1)S(1)}, bf16[24,1728]{1,0:T(8,128)(2,1)S(1)}, u32[]{:S(2)}, u32[]{:S(2)}) collective-permute-start(bf16[24,1728]{1,0:T(8,128)(2,1)S(1)} %get-tuple-element.9), channel_id=1, source_target_pairs={{0,96},{1,97},{2,98},{3,99},{4,100},{5,101},{6,102},{7,103},{8,104... | collective-permute-start | bytes 248840 | tf_op jit(solution)/shard_map/ppermute | solution.py:166
  204.2 1.0 collective-permute-start.21
  205.2 2.9 %collective-permute-start.20 = (bf16[24,1728]{1,0:T(8,128)(2,1)S(1)}, bf16[24,1728]{1,0:T(8,128)(2,1)S(1)}, u32[]{:S(2)}, u32[]{:S(2)}) collective-permute-start(bf16[24,1728]{1,0:T(8,128)(2,1)S(1)} %get-tuple-element.11), channel_id=1, source_target_pairs={{0,80},{1,81},{2,82},{3,83},{4,84},{5,85},{6,86},{7,87},{8,88},{9,... | collective-permute-start | bytes 248840 | tf_op jit(solution)/shard_map/ppermute | solution.py:166
  208.1 0.3 collective-permute-start.19
  208.4 2.4 %collective-permute-start.18 = (bf16[24,1728]{1,0:T(8,128)(2,1)S(1)}, bf16[24,1728]{1,0:T(8,128)(2,1)S(1)}, u32[]{:S(2)}, u32[]{:S(2)}) collective-permute-start(bf16[24,1728]{1,0:T(8,128)(2,1)S(1)} %get-tuple-element.13), channel_id=1, source_target_pairs={{0,48},{1,49},{2,50},{3,51},{4,52},{5,53},{6,54},{7,55},{8,56},{9,... | collective-permute-start | bytes 248840 | tf_op jit(solution)/shard_map/ppermute | solution.py:166
  210.8 0.7 collective-permute-start.16
  211.5 0.7 collective-permute-done.20
  212.2 1.1 collective-permute-done.19
  213.2 0.7 collective-permute-done.18
  213.9 1.9 collective-permute-done.17
  215.9 2.3 %fusion.9 = f32[3,64,1728]{2,1,0:T(8,128)} fusion(bf16[24,1728]{1,0:T(8,128)(2,1)S(1)} %collective-permute-done.22, bf16[24,1728]{1,0:T(8,128)(2,1)S(1)} %collective-permute-done.21, bf16[24,1728]{1,0:T(8,128)(2,1)S(1)} %collective-permute-done.20, bf16[24,1728]{1,0:T(8,128)(2,1)S(1)} %collective-permute-done.19, ...), kind=kOutput, calls=%fused_computation.15 | convolution fusion | flops 32474112 | bytes 2027524 | tf_op jit(solution)/shard_map/ckf,ckj->cjf/dot_general | solution.py:209
  (27 shorter events, 0.2 us)
Async XLA Ops:
  7.2 165.3 %all-gather.2.cloned.1.call-start = ((), (), s32[]{:S(2)}) async-start(), calls=%async_computation.1 | async-start | bytes 3538944 | tf_op jit(solution)/shard_map/all_gather | solution.py:200
  7.2 19.9 %collective-permute-start.1 = (bf16[192,1728]{1,0:T(8,128)(2,1)}, bf16[192,1728]{1,0:T(8,128)(2,1)S(1)}, u32[]{:S(2)}, u32[]{:S(2)}) collective-permute-start(bf16[192,1728]{1,0:T(8,128)(2,1)} %bitcast.49), channel_id=1, source_target_pairs={{0,64},{1,65},{2,66},{3,67},{4,68},{5,69},{6,70},{7,71},{8,72},{9,... | collective-permute-start | bytes 1990664 | tf_op jit(solution)/shard_map/ppermute | solution.py:166
  11.7 17.4 %collective-permute-start.3 = (bf16[192,1728]{1,0:T(8,128)(2,1)}, bf16[192,1728]{1,0:T(8,128)(2,1)S(1)}, u32[]{:S(2)}, u32[]{:S(2)}) collective-permute-start(bf16[192,1728]{1,0:T(8,128)(2,1)} %bitcast.50), channel_id=1, source_target_pairs={{0,48},{1,49},{2,50},{3,51},{4,52},{5,53},{6,54},{7,55},{8,56},{9,... | collective-permute-start | bytes 1990664 | tf_op jit(solution)/shard_map/ppermute | solution.py:166
  14.2 30.7 %collective-permute-start = (bf16[192,1728]{1,0:T(8,128)(2,1)}, bf16[192,1728]{1,0:T(8,128)(2,1)S(1)}, u32[]{:S(2)}, u32[]{:S(2)}) collective-permute-start(bf16[192,1728]{1,0:T(8,128)(2,1)} %bitcast.51), channel_id=1, source_target_pairs={{0,8},{1,9},{2,10},{3,11},{4,12},{5,13},{6,14},{7,15},{8,0},{9,1},... | collective-permute-start | bytes 1990664 | tf_op jit(solution)/shard_map/ppermute | solution.py:166
  15.4 33.2 %collective-permute-start.5 = (bf16[192,1728]{1,0:T(8,128)(2,1)}, bf16[192,1728]{1,0:T(8,128)(2,1)S(1)}, u32[]{:S(2)}, u32[]{:S(2)}) collective-permute-start(bf16[192,1728]{1,0:T(8,128)(2,1)} %bitcast.52), channel_id=1, source_target_pairs={{0,16},{1,17},{2,18},{3,19},{4,20},{5,21},{6,22},{7,23},{8,24},{9,... | collective-permute-start | bytes 1990664 | tf_op jit(solution)/shard_map/ppermute | solution.py:166
  15.4 33.2 %collective-permute-start.7 = (bf16[192,1728]{1,0:T(8,128)(2,1)}, bf16[192,1728]{1,0:T(8,128)(2,1)}, u32[]{:S(2)}, u32[]{:S(2)}) collective-permute-start(bf16[192,1728]{1,0:T(8,128)(2,1)} %bitcast.53), channel_id=1, source_target_pairs={{0,32},{1,33},{2,34},{3,35},{4,36},{5,37},{6,38},{7,39},{8,40},{9,... | collective-permute-start | bytes 1990664 | tf_op jit(solution)/shard_map/ppermute | solution.py:166
  27.1 21.6 %collective-permute-start.2 = (bf16[192,1728]{1,0:T(8,128)(2,1)S(1)}, bf16[192,1728]{1,0:T(8,128)(2,1)S(1)}, u32[]{:S(2)}, u32[]{:S(2)}) collective-permute-start(bf16[192,1728]{1,0:T(8,128)(2,1)S(1)} %collective-permute-done.1.refs_2_), channel_id=1, source_target_pairs={{0,8},{1,9},{2,10},{3,11},{4,12},{5,13},{6,14},{7,15},{8,0},{9,1},... | collective-permute-start | bytes 1990664 | tf_op jit(solution)/shard_map/ppermute | solution.py:166
  29.1 21.3 %collective-permute-start.4 = (bf16[192,1728]{1,0:T(8,128)(2,1)S(1)}, bf16[192,1728]{1,0:T(8,128)(2,1)S(1)}, u32[]{:S(2)}, u32[]{:S(2)}) collective-permute-start(bf16[192,1728]{1,0:T(8,128)(2,1)S(1)} %collective-permute-done.3.refs_4_), channel_id=1, source_target_pairs={{0,8},{1,9},{2,10},{3,11},{4,12},{5,13},{6,14},{7,15},{8,0},{9,1},... | collective-permute-start | bytes 1990664 | tf_op jit(solution)/shard_map/ppermute | solution.py:166
  44.9 18.1 %collective-permute-start.9 = (bf16[192,1728]{1,0:T(8,128)(2,1)S(1)}, bf16[192,1728]{1,0:T(8,128)(2,1)}, u32[]{:S(2)}, u32[]{:S(2)}) collective-permute-start(bf16[192,1728]{1,0:T(8,128)(2,1)S(1)} %collective-permute-done.1.refs_2_), channel_id=1, source_target_pairs={{0,48},{1,49},{2,50},{3,51},{4,52},{5,53},{6,54},{7,55},{8,56},{9,... | collective-permute-start | bytes 1990664 | tf_op jit(solution)/shard_map/ppermute | solution.py:166
  48.7 17.5 %collective-permute-start.11 = (bf16[192,1728]{1,0:T(8,128)(2,1)S(1)}, bf16[192,1728]{1,0:T(8,128)(2,1)}, u32[]{:S(2)}, u32[]{:S(2)}) collective-permute-start(bf16[192,1728]{1,0:T(8,128)(2,1)S(1)} %collective-permute-done.1.refs_2_), channel_id=1, source_target_pairs={{0,16},{1,17},{2,18},{3,19},{4,20},{5,21},{6,22},{7,23},{8,24},{9,... | collective-permute-start | bytes 1990664 | tf_op jit(solution)/shard_map/ppermute | solution.py:166
  48.7 19.2 %collective-permute-start.13 = (bf16[192,1728]{1,0:T(8,128)(2,1)}, bf16[192,1728]{1,0:T(8,128)(2,1)}, u32[]{:S(2)}, u32[]{:S(2)}) collective-permute-start(bf16[192,1728]{1,0:T(8,128)(2,1)} %collective-permute-done.7.refs_8_), channel_id=1, source_target_pairs={{0,64},{1,65},{2,66},{3,67},{4,68},{5,69},{6,70},{7,71},{8,72},{9,... | collective-permute-start | bytes 1990664 | tf_op jit(solution)/shard_map/ppermute | solution.py:166
  48.7 0.8 copy-start.2
  49.5 19.0 %collective-permute-start.8 = (bf16[192,1728]{1,0:T(8,128)(2,1)}, bf16[192,1728]{1,0:T(8,128)(2,1)}, u32[]{:S(2)}, u32[]{:S(2)}) collective-permute-start(bf16[192,1728]{1,0:T(8,128)(2,1)} %collective-permute-done.7.refs_8_), channel_id=1, source_target_pairs={{0,8},{1,9},{2,10},{3,11},{4,12},{5,13},{6,14},{7,15},{8,0},{9,1},... | collective-permute-start | bytes 1990664 | tf_op jit(solution)/shard_map/ppermute | solution.py:166
  50.4 0.8 copy-start.4
  51.2 17.3 %collective-permute-start.6 = (bf16[192,1728]{1,0:T(8,128)(2,1)S(1)}, bf16[192,1728]{1,0:T(8,128)(2,1)}, u32[]{:S(2)}, u32[]{:S(2)}) collective-permute-start(bf16[192,1728]{1,0:T(8,128)(2,1)S(1)} %collective-permute-done.5.refs_6_), channel_id=1, source_target_pairs={{0,8},{1,9},{2,10},{3,11},{4,12},{5,13},{6,14},{7,15},{8,0},{9,1},... | collective-permute-start | bytes 1990664 | tf_op jit(solution)/shard_map/ppermute | solution.py:166
  63.1 5.4 %collective-permute-start.10 = (bf16[192,1728]{1,0:T(8,128)(2,1)}, bf16[192,1728]{1,0:T(8,128)(2,1)}, u32[]{:S(2)}, u32[]{:S(2)}) collective-permute-start(bf16[192,1728]{1,0:T(8,128)(2,1)} %collective-permute-done.9.refs_10_), channel_id=1, source_target_pairs={{0,8},{1,9},{2,10},{3,11},{4,12},{5,13},{6,14},{7,15},{8,0},{9,1},... | collective-permute-start | bytes 1990664 | tf_op jit(solution)/shard_map/ppermute | solution.py:166
  66.2 3.8 %collective-permute-start.12 = (bf16[192,1728]{1,0:T(8,128)(2,1)}, bf16[192,1728]{1,0:T(8,128)(2,1)}, u32[]{:S(2)}, u32[]{:S(2)}) collective-permute-start(bf16[192,1728]{1,0:T(8,128)(2,1)} %collective-permute-done.11.refs_12_), channel_id=1, source_target_pairs={{0,8},{1,9},{2,10},{3,11},{4,12},{5,13},{6,14},{7,15},{8,0},{9,1},... | collective-permute-start | bytes 1990664 | tf_op jit(solution)/shard_map/ppermute | solution.py:166
  67.8 3.1 %collective-permute-start.14 = (bf16[192,1728]{1,0:T(8,128)(2,1)}, bf16[192,1728]{1,0:T(8,128)(2,1)}, u32[]{:S(2)}, u32[]{:S(2)}) collective-permute-start(bf16[192,1728]{1,0:T(8,128)(2,1)} %collective-permute-done.13.refs_14_), channel_id=1, source_target_pairs={{0,8},{1,9},{2,10},{3,11},{4,12},{5,13},{6,14},{7,15},{8,0},{9,1},... | collective-permute-start | bytes 1990664 | tf_op jit(solution)/shard_map/ppermute | solution.py:166
  70.9 1.1 copy-start.1
  72.0 1.1 copy-start.3
  73.1 1.1 copy-start.5
  74.2 1.0 copy-start.6
  129.7 3.2 %copy-start.7 = (s32[48,8]{0,1:T(8,128)S(1)}, s32[48,8]{0,1:T(8,128)}, u32[]{:S(2)}) copy-start(s32[48,8]{0,1:T(8,128)} %param.9) | copy-start | bytes 4612
  172.5 1.5 copy-start
  193.9 5.0 %collective-permute-start.15 = (bf16[8,24,1728]{2,1,0:T(8,128)(2,1)S(1)}, bf16[8,24,1728]{2,1,0:T(8,128)(2,1)S(1)}, u32[]{:S(2)}, u32[]{:S(2)}) collective-permute-start(bf16[8,24,1728]{2,1,0:T(8,128)(2,1)S(1)} %get-tuple-element.7), channel_id=1, source_target_pairs={{0,8},{1,9},{2,10},{3,11},{4,12},{5,13},{6,14},{7,15},{8,0},{9,1},... | collective-permute-start | bytes 1990664 | tf_op jit(solution)/shard_map/ppermute | solution.py:166
  199.2 11.6 %collective-permute-start.22 = (bf16[24,1728]{1,0:T(8,128)(2,1)S(1)}, bf16[24,1728]{1,0:T(8,128)(2,1)S(1)}, u32[]{:S(2)}, u32[]{:S(2)}) collective-permute-start(bf16[24,1728]{1,0:T(8,128)(2,1)S(1)} %get-tuple-element.9), channel_id=1, source_target_pairs={{0,96},{1,97},{2,98},{3,99},{4,100},{5,101},{6,102},{7,103},{8,104... | collective-permute-start | bytes 248840 | tf_op jit(solution)/shard_map/ppermute | solution.py:166
  204.2 6.6 %collective-permute-start.21 = (bf16[24,1728]{1,0:T(8,128)(2,1)S(1)}, bf16[24,1728]{1,0:T(8,128)(2,1)S(1)}, u32[]{:S(2)}, u32[]{:S(2)}) collective-permute-start(bf16[24,1728]{1,0:T(8,128)(2,1)S(1)} %get-tuple-element.10), channel_id=1, source_target_pairs={{0,112},{1,113},{2,114},{3,115},{4,116},{5,117},{6,118},{7,119},{8... | collective-permute-start | bytes 248840 | tf_op jit(solution)/shard_map/ppermute | solution.py:166
  205.2 7.0 %collective-permute-start.20 = (bf16[24,1728]{1,0:T(8,128)(2,1)S(1)}, bf16[24,1728]{1,0:T(8,128)(2,1)S(1)}, u32[]{:S(2)}, u32[]{:S(2)}) collective-permute-start(bf16[24,1728]{1,0:T(8,128)(2,1)S(1)} %get-tuple-element.11), channel_id=1, source_target_pairs={{0,80},{1,81},{2,82},{3,83},{4,84},{5,85},{6,86},{7,87},{8,88},{9,... | collective-permute-start | bytes 248840 | tf_op jit(solution)/shard_map/ppermute | solution.py:166
  208.1 5.1 %collective-permute-start.19 = (bf16[24,1728]{1,0:T(8,128)(2,1)S(1)}, bf16[24,1728]{1,0:T(8,128)(2,1)S(1)}, u32[]{:S(2)}, u32[]{:S(2)}) collective-permute-start(bf16[24,1728]{1,0:T(8,128)(2,1)S(1)} %get-tuple-element.12), channel_id=1, source_target_pairs={{0,32},{1,33},{2,34},{3,35},{4,36},{5,37},{6,38},{7,39},{8,40},{9,... | collective-permute-start | bytes 248840 | tf_op jit(solution)/shard_map/ppermute | solution.py:166
  208.4 5.6 %collective-permute-start.18 = (bf16[24,1728]{1,0:T(8,128)(2,1)S(1)}, bf16[24,1728]{1,0:T(8,128)(2,1)S(1)}, u32[]{:S(2)}, u32[]{:S(2)}) collective-permute-start(bf16[24,1728]{1,0:T(8,128)(2,1)S(1)} %get-tuple-element.13), channel_id=1, source_target_pairs={{0,48},{1,49},{2,50},{3,51},{4,52},{5,53},{6,54},{7,55},{8,56},{9,... | collective-permute-start | bytes 248840 | tf_op jit(solution)/shard_map/ppermute | solution.py:166
  210.8 5.1 %collective-permute-start.17 = (bf16[24,1728]{1,0:T(8,128)(2,1)S(1)}, bf16[24,1728]{1,0:T(8,128)(2,1)S(1)}, u32[]{:S(2)}, u32[]{:S(2)}) collective-permute-start(bf16[24,1728]{1,0:T(8,128)(2,1)S(1)} %get-tuple-element.14), channel_id=1, source_target_pairs={{0,16},{1,17},{2,18},{3,19},{4,20},{5,21},{6,22},{7,23},{8,24},{9,... | collective-permute-start | bytes 248840 | tf_op jit(solution)/shard_map/ppermute | solution.py:166
  210.8 5.1 %collective-permute-start.16 = (bf16[24,1728]{1,0:T(8,128)(2,1)S(1)}, bf16[24,1728]{1,0:T(8,128)(2,1)S(1)}, u32[]{:S(2)}, u32[]{:S(2)}) collective-permute-start(bf16[24,1728]{1,0:T(8,128)(2,1)S(1)} %get-tuple-element.8), channel_id=1, source_target_pairs={{0,64},{1,65},{2,66},{3,67},{4,68},{5,69},{6,70},{7,71},{8,72},{9,... | collective-permute-start | bytes 248840 | tf_op jit(solution)/shard_map/ppermute | solution.py:166
Sparse Core Ops, SparseCore 0:
  133.0 39.3 all-gather.1

commit v2 on v1

v2 whole, which is shorter than its diff:
```python
import functools
import math

import jax
import jax.numpy as jnp
from jax import lax
from jax.experimental import pallas as pl
from jax.experimental.pallas import tpu as pltpu
from jax.sharding import Mesh, PartitionSpec as P
import numpy as np

CL = 64
DECAY = 0.9
AXES = ("zh", "x", "c", "zl", "y")
DP = ("zh", "x", "c")
TENSOR = ("zl", "y")
ANY = pl.BlockSpec(memory_space=pl.ANY)
CHUNK_US = (4, 6)
TILE = 896
CHUNKS = (((0, 0), (1, 0), (0, 1), (0, 3)), ((0, 2), (1, 1), (1, 3), (1, 2)))


def cosine_table():
    freq_ids = jnp.arange(CL, dtype=jnp.float32)[:, None]
    cell_ids = jnp.arange(CL, dtype=jnp.float32)[None, :]
    scale_row = jnp.where(freq_ids == 0, math.sqrt(1.0 / CL), math.sqrt(2.0 / CL))
    return scale_row * jnp.cos(math.pi * (2.0 * cell_ids + 1.0) * freq_ids / (2.0 * CL))


def shift(sizes, **by):
    step = [by.get(a, 0) for a in AXES]
    pairs = []
    for at in np.ndindex(*sizes):
        to = [(a + s) % n for a, s, n in zip(at, step, sizes)]
        pairs.append((int(np.ravel_multi_index(at, sizes)), int(np.ravel_multi_index(to, sizes))))
    return pairs


def output_kernel(pieces, info, ht_ref, target_ref, *refs):
    blocks, (out_ref, w_ref, sems) = refs[:-3], refs[-3:]
    core = info[0]
    shards, n, rows, _ = out_ref.shape
    half = shards * rows // 2
    copies = []
    at = 0
    for k, count in enumerate(pieces):
        slot = core if k % 2 == 0 else 1 - core
        base = (k // 2 * 2 + slot) * half
        for _ in range(count):
            size = blocks[at].shape[0]
            to = pl.ds(pl.multiple_of(base, 16), size)
            copies.append((k // 2, pltpu.make_async_copy(blocks[at], w_ref.at[to], sems.at[at])))
            base = base + size
            at += 1
    for _, copy in copies:
        copy.start()
    for u in range(n):
        for unit, copy in copies:
            if unit == u:
                copy.wait()
        value = jnp.dot(
            w_ref[2 * u * half : 2 * (u + 1) * half], ht_ref[...], preferred_element_type=jnp.float32
        )
        for i in range(shards):
            out_ref[i, u] = value[i * rows : (i + 1) * rows].astype(jnp.bfloat16)

        @pl.when(info[1 + u] != 0)
        def _():
            goal = target_ref[...].astype(jnp.float32).T
            for i in range(shards):
                here = out_ref[i, u].astype(jnp.float32) - goal[i * rows : (i + 1) * rows]
                out_ref[i, u] = here.astype(jnp.bfloat16)


def partial_output(shards, info, ht, target, blocks, us):
    depth, count = ht.shape
    width = target.shape[1]
    n = len(blocks) // 2
    pieces = tuple(len(b) for b in blocks)
    blocks = [piece for b in blocks for piece in b]
    vmem = pl.BlockSpec(memory_space=pltpu.VMEM)
    return pl.pallas_call(
        functools.partial(output_kernel, pieces),
        out_shape=jax.ShapeDtypeStruct((shards, n, width // shards, count), jnp.bfloat16),
        in_specs=[pl.BlockSpec(memory_space=pltpu.SMEM), vmem, vmem] + [ANY] * len(blocks),
        out_specs=vmem,
        scratch_shapes=[
            pltpu.VMEM((n * width, depth), jnp.bfloat16),
            pltpu.SemaphoreType.DMA((len(blocks),)),
        ],
        compiler_params=pltpu.CompilerParams(vmem_limit_bytes=56 * 2**20),
        cost_estimate=pl.CostEstimate(flops=int(us * 10**9), bytes_accessed=1, transcendentals=0),
    )(info, ht, target, *blocks)


def residual_kernel(parts_ref, *refs):
    out_ref = refs[-1]
    for u in range(out_ref.shape[1]):
        total = jnp.sum(parts_ref[:, u].astype(jnp.float32), axis=0).astype(jnp.bfloat16)
        for k in range(out_ref.shape[0]):
            out_ref[k, u] = total


def residual_copies(parts, after):
    vmem = pl.BlockSpec(memory_space=pltpu.VMEM)
    return pl.pallas_call(
        residual_kernel,
        out_shape=jax.ShapeDtypeStruct(parts.shape, jnp.bfloat16),
        in_specs=[vmem] + [ANY] * len(after),
        out_specs=vmem,
        compiler_params=pltpu.CompilerParams(vmem_limit_bytes=48 * 2**20),
        cost_estimate=pl.CostEstimate(flops=parts.size, bytes_accessed=4 * parts.size, transcendentals=0),
    )(parts, *after)


def step_kernel(factor, info, ht_ref, rt_ref, m_ref, keep_ref, code_ref, *refs):
    new_ref, mine_ref, other_ref = refs[-3:]
    rows = m_ref.shape[0]
    width = m_ref.shape[1]
    mine = mine_ref.shape[0]
    rt = rt_ref[...].reshape(width, rt_ref.shape[2])
    keep = keep_ref[0]
    code = code_ref[0]
    for start in range(0, rows, TILE):
        size = min(TILE, rows - start)
        f = pl.ds(start, size)
        grad = lax.dot_general(
            ht_ref[f, :], rt, (((1,), (1,)), ((), ())), preferred_element_type=jnp.float32
        )
        primed = DECAY * m_ref[f, :].astype(jnp.float32) + grad * factor
        low = primed.astype(jnp.bfloat16)
        for a in range(0, width, 256):
            b = min(a + 256, width)
            gone = jnp.dot(low[:, a:b], keep[a:b, a:b], preferred_element_type=jnp.float32)
            new_ref[f, a:b] = (primed[:, a:b] - gone).astype(jnp.bfloat16)
        coeffs = lax.dot_general(
            code, low, (((1,), (1,)), ((), ())), preferred_element_type=jnp.float32
        ).astype(jnp.bfloat16)
        mine_ref[:, f] = coeffs[:mine]
        other_ref[:, f] = coeffs[mine:]


def momentum_step(chips, ht, rt, momentum, keep, code, state, factor):
    n = chips.shape[0]
    n_chips = code.shape[0]
    rows, width_all = momentum.shape
    tokens = ht.shape[1]
    shards, _, slab, _ = rt.shape
    width = shards * slab
    kept = code.shape[1]
    mine = kept // 2
    in_specs = [
        pl.BlockSpec((rows, tokens), lambda u, c: (0, 0)),
        pl.BlockSpec((shards, None, slab, tokens), lambda u, c: (0, u, 0, 0)),
        pl.BlockSpec((rows, width), lambda u, c: (0, c[u])),
        pl.BlockSpec((1, width, width), lambda u, c: (c[u], 0, 0)),
        pl.BlockSpec((1, kept, width), lambda u, c: (c[u], 0, 0)),
    ]
    args = [ht, rt, momentum, keep, code]
    alias = {}
    if state is not None:
        in_specs += [ANY] * 3
        args += state
        alias = {6: 0, 7: 1, 8: 2}
    return pl.pallas_call(
        functools.partial(step_kernel, factor),
        out_shape=(
            jax.ShapeDtypeStruct((rows, width_all), jnp.bfloat16),
            jax.ShapeDtypeStruct((n_chips, mine, rows), jnp.bfloat16),
            jax.ShapeDtypeStruct((n_chips, mine, rows), jnp.bfloat16),
        ),
        grid_spec=pltpu.PrefetchScalarGridSpec(
            num_scalar_prefetch=1,
            grid=(n,),
            in_specs=in_specs,
            out_specs=(
                pl.BlockSpec((rows, width), lambda u, c: (0, c[u])),
                pl.BlockSpec((None, mine, rows), lambda u, c: (c[u], 0, 0)),
                pl.BlockSpec((None, mine, rows), lambda u, c: (c[u], 0, 0)),
            ),
        ),
        input_output_aliases=alias,
        compiler_params=pltpu.CompilerParams(
            vmem_limit_bytes=60 * 2**20, dimension_semantics=("arbitrary",)
        ),
        cost_estimate=pl.CostEstimate(
            flops=2 * n * rows * width * (tokens + 256 + kept),
            bytes_accessed=2 * (2 * n * rows * width + rows * tokens),
            transcendentals=0,
        ),
    )(chips, *args)


def table_kernel(info, freqs_ref, cosines_ref, keep_ref, code_ref):
    rows, width = code_ref.shape[1:]
    per = width // CL
    kept = rows // per
    freqs = freqs_ref[0]
    onehot = (freqs == lax.broadcasted_iota(jnp.int32, (rows, CL), 1)).astype(jnp.float32)
    chosen = jnp.dot(
        onehot, cosines_ref[...], precision=lax.Precision.HIGHEST, preferred_element_type=jnp.float32
    )
    wide = jnp.concatenate([chosen] * per, axis=1)
    block = lax.broadcasted_iota(jnp.int32, (rows, width), 0) // kept + info[0] * (per // 2)
    block = jnp.where(block >= per, block - per, block)
    wide = jnp.where(block == lax.broadcasted_iota(jnp.int32, (rows, width), 1) // CL, wide, 0.0)
    code_ref[0] = wide.astype(jnp.bfloat16)
    keep_ref[...] = jnp.zeros(keep_ref.shape, jnp.bfloat16)
    for a in range(0, width, 128):
        tile = wide[:, a : a + 128]
        keep_ref[0, a : a + 128, a : a + 128] = lax.dot_general(
            tile,
            tile,
            (((0,), (0,)), ((), ())),
            precision=lax.Precision.HIGHEST,
            preferred_element_type=jnp.float32,
        ).astype(jnp.bfloat16)


def tables(freqs, core, n_chips):
    blocks, kept = freqs.shape
    per = blocks // n_chips
    ordered = freqs.reshape(n_chips, 2, per // 2 * kept)
    ordered = jnp.where(core == 0, ordered, ordered[:, ::-1]).reshape(n_chips, per * kept, 1)
    return pl.pallas_call(
        table_kernel,
        out_shape=(
            jax.ShapeDtypeStruct((n_chips, per * CL, per * CL), jnp.bfloat16),
            jax.ShapeDtypeStruct((n_chips, per * kept, per * CL), jnp.bfloat16),
        ),
        grid=(n_chips,),
        in_specs=[
            pl.BlockSpec(memory_space=pltpu.SMEM),
            pl.BlockSpec((1, per * kept, 1), lambda u: (u, 0, 0)),
            pl.BlockSpec((CL, CL), lambda u: (0, 0)),
        ],
        out_specs=(
            pl.BlockSpec((1, per * CL, per * CL), lambda u: (u, 0, 0)),
            pl.BlockSpec((1, per * kept, per * CL), lambda u: (u, 0, 0)),
        ),
        compiler_params=pltpu.CompilerParams(vmem_limit_bytes=32 * 2**20),
        cost_estimate=pl.CostEstimate(flops=10**9, bytes_accessed=4 * 10**6, transcendentals=0),
    )(core[None].astype(jnp.int32), ordered, cosine_table())


def per_device(sizes, hidden, weight, momentum, target, freqs):
    send = lambda v, **by: lax.ppermute(v, AXES, shift(sizes, **by))
    zh, x, c = (lax.axis_index(a) for a in DP)
    n_zh, n_x = sizes[0], sizes[1]
    n_tensor = sizes[3] * sizes[4]
    shard = lax.axis_index(TENSOR)
    n_chips = n_zh * n_x
    ht = hidden.T
    own = weight.T
    factor = 1.0 / math.sqrt(hidden.shape[0])

    cut = own.shape[0] // 2
    blocks = {(0, 0): [own], (1, 0): [send(own, zh=1)], (0, 1): [send(own, x=-1)], (0, 3): [send(own, x=1)]}
    for z in range(2):
        if z:
            blocks[z, 1] = [send(blocks[z, 0][0], x=-1)]
            blocks[z, 3] = [send(blocks[z, 0][0], x=1)]
        blocks[z, 2] = [send(blocks[z, 1][0][:cut], x=-1), send(blocks[z, 3][0][cut:], x=1)]
    swapped = {s: [send(piece, c=1) for piece in b] for s, b in blocks.items()}
    keep, code = tables(freqs, c, n_chips)

    core = c[None].astype(jnp.int32)
    chips, partials = [], []
    for chunk, us in zip(CHUNKS, CHUNK_US):
        at = jnp.stack([((zh + s[0]) % n_zh) * n_x + (x + s[1]) % n_x for s in chunk]).astype(jnp.int32)
        chips.append(at)
        partials.append(
            partial_output(
                n_tensor,
                jnp.concatenate([core, (at == shard).astype(jnp.int32)]),
                ht,
                target,
                [b for s in chunk for b in (blocks[s], swapped[s])],
                us,
            )
        )
    received = [lax.all_to_all(p, TENSOR, 0, 0) for p in partials]
    copies = [residual_copies(r, partials[i + 1 :]) for i, r in enumerate(received)]
    gathered = [lax.all_to_all(k, TENSOR, 0, 0) for k in copies]

    state = None
    for at, whole in zip(chips, gathered):
        state = momentum_step(at, ht, whole, momentum[0], keep, code, state, factor)
    state, mine, other = state

    pair = (mine.astype(jnp.float32) + send(other, c=1).astype(jnp.float32)).astype(jnp.bfloat16)
    total = jnp.sum(lax.all_to_all(pair, ("zh", "x"), 0, 0).astype(jnp.float32), axis=0)
    n_dp = n_chips * sizes[2]
    per = freqs.shape[0] // n_dp
    own_freqs = lax.dynamic_slice_in_dim(freqs, lax.axis_index(DP) * per, per, 0)
    onehot = (own_freqs[:, :, None] == jnp.arange(CL, dtype=jnp.int32)).astype(jnp.float32)
    own_basis = jnp.einsum("ckv,vj->ckj", onehot, cosine_table(), precision=lax.Precision.HIGHEST)
    decoded = jnp.einsum(
        "ckf,ckj->cjf",
        total.reshape(per, total.shape[0] // per, total.shape[1]),
        own_basis * (1.0 / n_dp),
        precision=lax.Precision.HIGHEST,
    )
    return state[None], decoded.reshape(per * CL, -1).T


def solution(mesh):
    sizes = (2, 4, 2, 2, 4)
    fine = Mesh(mesh.devices.reshape(sizes), AXES)
    in_specs = (P(DP, TENSOR), P(TENSOR, DP), P(DP, TENSOR, None), P(DP, TENSOR), P())
    out_specs = (P(DP, TENSOR, None), P(TENSOR, DP))
    return jax.shard_map(
        functools.partial(per_device, sizes),
        mesh=fine,
        in_specs=in_specs,
        out_specs=out_specs,
        check_vma=False,
    )
```

time: 227 us -> 191 us (0.84)
  blocking collectives: 42.3 us -> 0 us
  waiting for transfers between devices: 50.2 us -> 85.3 us
  local copies, waits for them, and re-layouts: 24.8 us -> 8.63 us
  Pallas kernels: 32.1 us -> 45.7 us
  between operations: 14.2 us -> 0.86 us
  starting transfers between devices: 49.8 us -> 42.5 us
  matrix products: 5.34 us -> 2.61 us
    all_to_all x0 -> x5, waiting for transfers between devices: none -> 53.4 us  [the longest x2 21.7 us: per_device(): gathered = [lax.all_to_all(k, TENSOR, 0, 0) for k in copies]]
    all_to_all x1 -> x0, blocking collectives: 42.3 us -> none  [per_device(): received = lax.all_to_all(split, TENSOR, 0, 0)]
    ppermute x23 -> x20, starting transfers between devices: 49.7 us -> 22.4 us  [per_device(): send = lambda v, **by: lax.ppermute(v, AXES, shift(sizes, **by))]
    all_to_all x0 -> x5, starting transfers between devices: none -> 20 us  [the longest x2 9.31 us: per_device(): received = [lax.all_to_all(p, TENSOR, 0, 0) for p in partials]]
    mul x8 -> x0, local copies, waits for them, and re-layouts: 17.1 us -> none  [the longest x4 16.4 us: tables(): proj = proj.reshape(n_chips, per, CL, 1, CL) * same[None, :, None, :, None]]
    all_gather x1 -> x0, waiting for transfers between devices: 16.3 us -> none  [per_device(): gathered = lax.all_gather(residual, TENSOR, axis=0, tiled=True)]
    pallas_call x2 -> x7, Pallas kernels: 32.1 us -> 45.7 us  [the longest x2 22.9 us: momentum_step(): pl.pallas_call(functools.partial(step_kernel, factor), out_shape=(jax.Sha...]
    reduce_sum x1, other arithmetic: 3.19 us -> 0.1 us  [per_device(): jnp.sum(lax.all_to_all(pair, ('zh', 'x'), 0, 0).astype(jnp.float32), axis=0)]
  transfers between devices with their start and end apart: 24 -> 25, of which waited for: 13 -> 11; matrix products, arithmetic and copies ran while one was open for 10% -> 2% of each run, Pallas kernels for 0% -> 18%
where the time goes in v2:
time: 191 us
  waiting for transfers between devices  85.3 us (45%)
  Pallas kernels  45.7 us (24%)
  starting transfers between devices  42.5 us (22%)
  local copies, waits for them, and re-layouts  8.63 us (5%)
  other arithmetic  5 us (3%)
  matrix products  2.61 us (1%)
    ppermute x20, waiting for transfers between devices, per_device(): send = lambda v, **by: lax.ppermute(v, AXES, shift(sizes, **by))  31.9 us
    pallas_call x2, Pallas kernels, momentum_step(): pl.pallas_call(functools.partial(step_kernel, factor), out_shape=(jax.Sha...  22.9 us
    ppermute x20, starting transfers between devices, per_device(): send = lambda v, **by: lax.ppermute(v, AXES, shift(sizes, **by))  22.4 us
    all_to_all x2, waiting for transfers between devices, per_device(): gathered = [lax.all_to_all(k, TENSOR, 0, 0) for k in copies]  21.7 us
    all_to_all x2, waiting for transfers between devices, per_device(): received = [lax.all_to_all(p, TENSOR, 0, 0) for p in partials]  18.6 us
    pallas_call x2, Pallas kernels, partial_output(): pl.pallas_call(functools.partial(output_kernel, pieces), out_shape=jax.Sh...  15.7 us
    all_to_all x1, waiting for transfers between devices, per_device(): lax.all_to_all(pair, ('zh', 'x'), 0, 0).astype(jnp.float32)  13 us
    all_to_all x2, starting transfers between devices, per_device(): received = [lax.all_to_all(p, TENSOR, 0, 0) for p in partials]  9.31 us
  transfers between devices with their start and end apart: 25, of which 11 were waited for; matrix products, arithmetic and copies ran while one was open for 2% of the time, Pallas kernels for 18%

profile of v2, /device:TPU:1, one launch (start us, length us, event | category | flops | bytes accessed | tf_op | source)
XLA Modules:
  0.0 190.5 jit_solution(4692754378343356609)
XLA Ops:
  0.6 4.5 %collective-permute-start.6 = (bf16[192,1728]{1,0:T(8,128)(2,1)}, bf16[192,1728]{1,0:T(8,128)(2,1)}, u32[]{:S(2)}, u32[]{:S(2)}) collective-permute-start(bf16[192,1728]{1,0:T(8,128)(2,1)} %bitcast.37), channel_id=1, source_target_pairs={{0,64},{1,65},{2,66},{3,67},{4,68},{5,69},{6,70},{7,71},{8,72},{9,... | collective-permute-start | bytes 1990664 | tf_op jit(solution)/shard_map/ppermute | solution.py:247
  5.1 2.5 %collective-permute-start = (bf16[192,1728]{1,0:T(8,128)(2,1)}, bf16[192,1728]{1,0:T(8,128)(2,1)S(1)}, u32[]{:S(2)}, u32[]{:S(2)}) collective-permute-start(bf16[192,1728]{1,0:T(8,128)(2,1)} %bitcast.38), channel_id=1, source_target_pairs={{0,48},{1,49},{2,50},{3,51},{4,52},{5,53},{6,54},{7,55},{8,56},{9,... | collective-permute-start | bytes 1990664 | tf_op jit(solution)/shard_map/ppermute | solution.py:247
  7.6 0.0 collective-permute-start.2
  7.6 1.2 collective-permute-start.15
  8.9 11.8 %collective-permute-done.6.refs_2_ = bf16[192,1728]{1,0:T(8,128)(2,1)} collective-permute-done((bf16[192,1728]{1,0:T(8,128)(2,1)}, bf16[192,1728]{1,0:T(8,128)(2,1)}, u32[]{:S(2)}, u32[]{:S(2)}) %collective-permute-start.6) | collective-permute-done | bytes 663584 | tf_op jit(solution)/shard_map/ppermute | solution.py:247
  20.6 1.2 collective-permute-start.16
  21.8 1.7 collective-permute-start.17
  23.6 1.1 collective-permute-done.2.refs_6_
  24.7 2.2 %collective-permute-start.18 = (bf16[192,1728]{1,0:T(8,128)(2,1)S(1)}, bf16[192,1728]{1,0:T(8,128)(2,1)}, u32[]{:S(2)}, u32[]{:S(2)}) collective-permute-start(bf16[192,1728]{1,0:T(8,128)(2,1)S(1)} %collective-permute-done.2.refs_6_), channel_id=1, source_target_pairs={{0,8},{1,9},{2,10},{3,11},{4,12},{5,13},{6,14},{7,15},{8,0},{9,1},... | collective-permute-start | bytes 1990664 | tf_op jit(solution)/shard_map/ppermute | solution.py:247
  26.9 0.1 collective-permute-start.7
  27.0 1.3 collective-permute-start.9
  28.4 0.6 compare_convert_fusion
  29.0 0.7 pad_add_fusion.3.info
  29.7 1.4 collective-permute-start.1
  31.2 0.1 collective-permute-start.3
  31.3 7.8 %shard_map.71 = bf16[8,4,48,512]{3,2,1,0:T(8,128)(2,1)} custom-call(s32[5]{0:T(128)} %pad_add_fusion.3.info, bf16[1728,512]{1,0:T(8,128)(2,1)} %bitcast.29, bf16[512,384]{1,0:T(8,128)(2,1)} %target_ref.3, bf16[192,1728]{1,0:T(8,128)(2,1)} %bitcast.41, bf16[192,1728]{1,0:T(8,128)(2,1)} %copy-done.10, bf16[192,1728]{1,0:T(8,128)(2,1)} %collective-permute-done.6.refs_2_, ...), custom_call_target="tpu_custom_call" | custom-call | flops 4000000000 | bytes 1 | tf_op jit(solution)/shard_map/pallas_call | solution.py:82
  39.1 4.5 %all-to-all-start.2 = ((bf16[8,4,48,512]{3,2,1,0:T(8,128)(2,1)}), bf16[8,4,48,512]{3,2,1,0:T(8,128)(2,1)S(1)}, u32[]{:S(2)}, u32[]{:S(2)}) async-start(bf16[8,4,48,512]{3,2,1,0:T(8,128)(2,1)} %shard_map.71), calls=%async_computation.2 | async-start | bytes 3145728 | tf_op jit(solution)/shard_map/all_to_all | solution.py:282
  43.6 8.0 %collective-permute-done.1.refs_0_ = bf16[96,1728]{1,0:T(8,128)(2,1)S(1)} collective-permute-done((bf16[96,1728]{1,0:T(8,128)(2,1)S(1)}, bf16[96,1728]{1,0:T(8,128)(2,1)S(1)}, u32[]{:S(2)}, u32[]{:S(2)}) %collective-permute-start.1) | collective-permute-done | bytes 331808 | tf_op jit(solution)/shard_map/ppermute | solution.py:247
  51.6 0.7 collective-permute-start.4
  52.4 1.4 collective-permute-start.11
  53.8 1.0 slice.19
  54.8 0.2 collective-permute-start.12
  55.0 0.6 collective-permute-start.10
  55.6 0.0 collective-permute-start.8
  55.6 0.5 collective-permute-start.5
  56.1 6.1 %collective-permute-done.11.refs_8_ = bf16[96,1728]{1,0:T(8,128)(2,1)} collective-permute-done((bf16[96,1728]{1,0:T(8,128)(2,1)S(1)}, bf16[96,1728]{1,0:T(8,128)(2,1)}, u32[]{:S(2)}, u32[]{:S(2)}) %collective-permute-start.11) | collective-permute-done | bytes 331808 | tf_op jit(solution)/shard_map/ppermute | solution.py:247
  62.2 0.8 collective-permute-start.13
  63.0 2.5 %collective-permute-done.12.refs_9_ = bf16[96,1728]{1,0:T(8,128)(2,1)} collective-permute-done((bf16[96,1728]{1,0:T(8,128)(2,1)S(1)}, bf16[96,1728]{1,0:T(8,128)(2,1)}, u32[]{:S(2)}, u32[]{:S(2)}) %collective-permute-start.12) | collective-permute-done | bytes 331808 | tf_op jit(solution)/shard_map/ppermute | solution.py:247
  65.5 1.1 collective-permute-start.14
  66.6 0.7 compare_convert_fusion.1
  67.3 0.7 pad_add_fusion.1.info
  68.0 0.3 collective-permute-done.14.refs_11_
  68.3 7.8 %shard_map.68.refs_0_ = bf16[8,4,48,512]{3,2,1,0:T(8,128)(2,1)} custom-call(s32[5]{0:T(128)} %pad_add_fusion.1.info, bf16[1728,512]{1,0:T(8,128)(2,1)} %bitcast.30, bf16[512,384]{1,0:T(8,128)(2,1)} %target_ref.3, bf16[96,1728]{1,0:T(8,128)(2,1)} %copy-done.11, bf16[96,1728]{1,0:T(8,128)(2,1)} %collective-permute-done.3.refs_1_, bf16[96,1728]{1,0:T(8,128)(2,1)} %copy-done.12, ...), custom_call_target="tpu_custom_call" | custom-call | flops 6000000000 | bytes 1 | tf_op jit(solution)/shard_map/pallas_call | solution.py:82
  76.1 4.8 %all-to-all-start = ((bf16[8,4,48,512]{3,2,1,0:T(8,128)(2,1)}), bf16[8,4,48,512]{3,2,1,0:T(8,128)(2,1)S(1)}, u32[]{:S(2)}, u32[]{:S(2)}) async-start(bf16[8,4,48,512]{3,2,1,0:T(8,128)(2,1)} %shard_map.68.refs_0_), calls=%async_computation | async-start | bytes 3145728 | tf_op jit(solution)/shard_map/all_to_all | solution.py:282
  81.0 1.4 copy-done.1
  82.4 0.2 shard_map.72
  82.6 1.2 copy-done.2
  83.8 18.6 %all-to-all-done.parts_ref = bf16[8,4,48,512]{3,2,1,0:T(8,128)(2,1)S(1)} async-done(((bf16[8,4,48,512]{3,2,1,0:T(8,128)(2,1)}), bf16[8,4,48,512]{3,2,1,0:T(8,128)(2,1)S(1)}, u32[]{:S(2)}, u32[]{:S(2)}) %all-to-all-start) | async-done | bytes 1572896 | tf_op jit(solution)/shard_map/all_to_all | solution.py:282
  102.4 3.6 %all-to-all-start.3 = ((bf16[8,4,48,512]{3,2,1,0:T(8,128)(2,1)}), bf16[8,4,48,512]{3,2,1,0:T(8,128)(2,1)S(1)}, u32[]{:S(2)}, u32[]{:S(2)}) async-start(bf16[8,4,48,512]{3,2,1,0:T(8,128)(2,1)} %copy-done.2), calls=%async_computation.3 | async-start | bytes 3145728 | tf_op jit(solution)/shard_map/all_to_all | solution.py:284
  106.0 1.3 shard_map.69
  107.4 20.0 %all-to-all-done.3.rt_ref = bf16[8,4,48,512]{3,2,1,0:T(8,128)(2,1)S(1)} async-done(((bf16[8,4,48,512]{3,2,1,0:T(8,128)(2,1)}), bf16[8,4,48,512]{3,2,1,0:T(8,128)(2,1)S(1)}, u32[]{:S(2)}, u32[]{:S(2)}) %all-to-all-start.3) | async-done | bytes 1572896 | tf_op jit(solution)/shard_map/all_to_all | solution.py:284
  127.4 1.2 copy-done.5
  128.6 3.6 %all-to-all-start.1 = ((bf16[8,4,48,512]{3,2,1,0:T(8,128)(2,1)}), bf16[8,4,48,512]{3,2,1,0:T(8,128)(2,1)S(1)}, u32[]{:S(2)}, u32[]{:S(2)}) async-start(bf16[8,4,48,512]{3,2,1,0:T(8,128)(2,1)} %shard_map.69), calls=%async_computation.1 | async-start | bytes 3145728 | tf_op jit(solution)/shard_map/all_to_all | solution.py:284
  132.2 0.1 copy.11
  132.2 0.1 reshape.33
  132.4 0.1 reshape.38.freqs_ref
  132.5 0.1 cosine_multiply_fusion.cosines_ref
  132.7 5.6 %shard_map.70 = (bf16[8,384,384]{2,1,0:T(8,128)(2,1)S(1)}, bf16[8,48,384]{2,1,0:T(8,128)(2,1)S(1)}) custom-call(s32[1]{0:T(128)} %bitcast.5.info, s32[8,48,1]{2,1,0:T(8,128)S(1)} %reshape.38.freqs_ref, f32[64,64]{1,0:T(8,128)S(1)} %cosine_multiply_fusion.cosines_ref), custom_call_target="tpu_custom_call" | custom-call | flops 1000000000 | bytes 4000000 | tf_op jit(solution)/shard_map/pallas_call | solution.py:225
  138.2 1.4 copy-done
  139.7 0.7 copy-done.3
  140.4 11.5 %shard_map.73 = (bf16[1728,3072]{1,0:T(8,128)(2,1)}, bf16[8,24,1728]{2,1,0:T(8,128)(2,1)}, bf16[8,24,1728]{2,1,0:T(8,128)(2,1)}) custom-call(s32[4]{0:T(128)} %get-tuple-element.19.info, bf16[1728,512]{1,0:T(8,128)(2,1)} %bitcast.31, bf16[8,4,48,512]{3,2,1,0:T(8,128)(2,1)} %copy-done.5, bf16[1728,3072]{1,0:T(8,128)(2,1)} %bitcast.26, ...), custom_call_target="tpu_custom_call" | custom-call | flops 4331667456 | bytes 12386304 | tf_op jit(solution)/shard_map/pallas_call | solution.py:165
  151.8 1.7 all-to-all-done.1.rt_ref
  153.5 1.1 copy-done.4
  154.7 11.5 %shard_map.74 = (bf16[1728,3072]{1,0:T(8,128)(2,1)}, bf16[8,24,1728]{2,1,0:T(8,128)(2,1)}, bf16[8,24,1728]{2,1,0:T(8,128)(2,1)}) custom-call(s32[4]{0:T(128)} %get-tuple-element.21.info, bf16[1728,512]{1,0:T(8,128)(2,1)} %bitcast.32, bf16[8,4,48,512]{3,2,1,0:T(8,128)(2,1)} %copy-done.4, ...), custom_call_target="tpu_custom_call", output_to_operand_aliasing={{0}: (6, {}), {1}: (7, {}), {2}: (8, {})} | custom-call | flops 4331667456 | bytes 12386304 | tf_op jit(solution)/shard_map/pallas_call | solution.py:165
  166.2 0.8 collective-permute-start.19
  167.0 2.0 %collective-permute-done.19 = bf16[8,24,1728]{2,1,0:T(8,128)(2,1)S(1)} collective-permute-done((bf16[8,24,1728]{2,1,0:T(8,128)(2,1)}, bf16[8,24,1728]{2,1,0:T(8,128)(2,1)S(1)}, u32[]{:S(2)}, u32[]{:S(2)}) %collective-permute-start.19) | collective-permute-done | bytes 663584 | tf_op jit(solution)/shard_map/ppermute | solution.py:247
  169.0 2.1 %add_convert_fusion = bf16[8,24,1728]{2,1,0:T(8,128)(2,1)} fusion(bf16[8,24,1728]{2,1,0:T(8,128)(2,1)S(1)} %collective-permute-done.19, bf16[8,24,1728]{2,1,0:T(8,128)(2,1)} %get-tuple-element.16), kind=kLoop, calls=%fused_computation.1 | loop fusion | flops 1327104 | bytes 1990656 | tf_op jit(solution)/shard_map/convert_element_type | solution.py:291
  171.1 3.5 %all-to-all-start.4 = ((bf16[8,24,1728]{2,1,0:T(8,128)(2,1)}), bf16[8,24,1728]{2,1,0:T(8,128)(2,1)S(1)}, u32[]{:S(2)}, u32[]{:S(2)}) async-start(bf16[8,24,1728]{2,1,0:T(8,128)(2,1)} %add_convert_fusion), calls=%async_computation.4 | async-start | bytes 1376256 | tf_op jit(solution)/shard_map/all_to_all | solution.py:292
  174.6 0.1 constant_dynamic-slice_fusion
  174.7 0.1 copy.13
  174.8 0.3 convolution_multiply_fusion
  175.1 13.0 %all-to-all-done.4 = bf16[8,24,1728]{2,1,0:T(8,128)(2,1)S(1)} async-done(((bf16[8,24,1728]{2,1,0:T(8,128)(2,1)}), bf16[8,24,1728]{2,1,0:T(8,128)(2,1)S(1)}, u32[]{:S(2)}, u32[]{:S(2)}) %all-to-all-start.4) | async-done | bytes 663584 | tf_op jit(solution)/shard_map/all_to_all | solution.py:292
  188.1 0.1 convert_reduce_fusion
  188.2 2.3 %fusion = f32[3,64,1728]{2,1,0:T(8,128)} fusion(f32[3,8,64]{2,1,0:T(8,128)S(1)} %convolution_multiply_fusion, f32[24,1728]{1,0:T(8,128)S(1)} %convert_reduce_fusion), kind=kOutput, calls=%fused_computation.3 | convolution fusion | flops 31850496 | bytes 1499136 | tf_op jit(solution)/shard_map/ckf,ckj->cjf/dot_general | solution.py:298
  (40 shorter events, 0.2 us)
Async XLA Ops:
  0.6 20.0 %collective-permute-start.6 = (bf16[192,1728]{1,0:T(8,128)(2,1)}, bf16[192,1728]{1,0:T(8,128)(2,1)}, u32[]{:S(2)}, u32[]{:S(2)}) collective-permute-start(bf16[192,1728]{1,0:T(8,128)(2,1)} %bitcast.37), channel_id=1, source_target_pairs={{0,64},{1,65},{2,66},{3,67},{4,68},{5,69},{6,70},{7,71},{8,72},{9,... | collective-permute-start | bytes 1990664 | tf_op jit(solution)/shard_map/ppermute | solution.py:247
  5.1 16.7 %collective-permute-start = (bf16[192,1728]{1,0:T(8,128)(2,1)}, bf16[192,1728]{1,0:T(8,128)(2,1)S(1)}, u32[]{:S(2)}, u32[]{:S(2)}) collective-permute-start(bf16[192,1728]{1,0:T(8,128)(2,1)} %bitcast.38), channel_id=1, source_target_pairs={{0,48},{1,49},{2,50},{3,51},{4,52},{5,53},{6,54},{7,55},{8,56},{9,... | collective-permute-start | bytes 1990664 | tf_op jit(solution)/shard_map/ppermute | solution.py:247
  7.6 17.1 %collective-permute-start.2 = (bf16[192,1728]{1,0:T(8,128)(2,1)}, bf16[192,1728]{1,0:T(8,128)(2,1)S(1)}, u32[]{:S(2)}, u32[]{:S(2)}) collective-permute-start(bf16[192,1728]{1,0:T(8,128)(2,1)} %bitcast.39), channel_id=1, source_target_pairs={{0,16},{1,17},{2,18},{3,19},{4,20},{5,21},{6,22},{7,23},{8,24},{9,... | collective-permute-start | bytes 1990664 | tf_op jit(solution)/shard_map/ppermute | solution.py:247
  7.6 19.4 %collective-permute-start.15 = (bf16[192,1728]{1,0:T(8,128)(2,1)}, bf16[192,1728]{1,0:T(8,128)(2,1)S(1)}, u32[]{:S(2)}, u32[]{:S(2)}) collective-permute-start(bf16[192,1728]{1,0:T(8,128)(2,1)} %bitcast.40), channel_id=1, source_target_pairs={{0,8},{1,9},{2,10},{3,11},{4,12},{5,13},{6,14},{7,15},{8,0},{9,1},... | collective-permute-start | bytes 1990664 | tf_op jit(solution)/shard_map/ppermute | solution.py:247
  20.6 9.1 %collective-permute-start.16 = (bf16[192,1728]{1,0:T(8,128)(2,1)}, bf16[192,1728]{1,0:T(8,128)(2,1)}, u32[]{:S(2)}, u32[]{:S(2)}) collective-permute-start(bf16[192,1728]{1,0:T(8,128)(2,1)} %collective-permute-done.6.refs_2_), channel_id=1, source_target_pairs={{0,8},{1,9},{2,10},{3,11},{4,12},{5,13},{6,14},{7,15},{8,0},{9,1},... | collective-permute-start | bytes 1990664 | tf_op jit(solution)/shard_map/ppermute | solution.py:247
  21.8 9.4 %copy-start.6 = (bf16[192,1728]{1,0:T(8,128)(2,1)}, bf16[192,1728]{1,0:T(8,128)(2,1)S(1)}, u32[]{:S(2)}) copy-start(bf16[192,1728]{1,0:T(8,128)(2,1)S(1)} %collective-permute-done.refs_4_) | copy-start | bytes 1990660
  21.8 9.3 %collective-permute-start.17 = (bf16[192,1728]{1,0:T(8,128)(2,1)S(1)}, bf16[192,1728]{1,0:T(8,128)(2,1)}, u32[]{:S(2)}, u32[]{:S(2)}) collective-permute-start(bf16[192,1728]{1,0:T(8,128)(2,1)S(1)} %collective-permute-done.refs_4_), channel_id=1, source_target_pairs={{0,8},{1,9},{2,10},{3,11},{4,12},{5,13},{6,14},{7,15},{8,0},{9,1},... | collective-permute-start | bytes 1990664 | tf_op jit(solution)/shard_map/ppermute | solution.py:247
  24.7 6.6 %copy-start.7 = (bf16[192,1728]{1,0:T(8,128)(2,1)}, bf16[192,1728]{1,0:T(8,128)(2,1)S(1)}, u32[]{:S(2)}) copy-start(bf16[192,1728]{1,0:T(8,128)(2,1)S(1)} %collective-permute-done.2.refs_6_) | copy-start | bytes 1990660
  24.7 6.6 %collective-permute-start.18 = (bf16[192,1728]{1,0:T(8,128)(2,1)S(1)}, bf16[192,1728]{1,0:T(8,128)(2,1)}, u32[]{:S(2)}, u32[]{:S(2)}) collective-permute-start(bf16[192,1728]{1,0:T(8,128)(2,1)S(1)} %collective-permute-done.2.refs_6_), channel_id=1, source_target_pairs={{0,8},{1,9},{2,10},{3,11},{4,12},{5,13},{6,14},{7,15},{8,0},{9,1},... | collective-permute-start | bytes 1990664 | tf_op jit(solution)/shard_map/ppermute | solution.py:247
  26.9 25.4 %collective-permute-start.7 = (bf16[192,1728]{1,0:T(8,128)(2,1)}, bf16[192,1728]{1,0:T(8,128)(2,1)S(1)}, u32[]{:S(2)}, u32[]{:S(2)}) collective-permute-start(bf16[192,1728]{1,0:T(8,128)(2,1)} %collective-permute-done.6.refs_2_), channel_id=1, source_target_pairs={{0,48},{1,49},{2,50},{3,51},{4,52},{5,53},{6,54},{7,55},{8,56},{9,... | collective-permute-start | bytes 1990664 | tf_op jit(solution)/shard_map/ppermute | solution.py:247
  27.0 1.3 copy-start.10
  27.0 26.7 %collective-permute-start.9 = (bf16[192,1728]{1,0:T(8,128)(2,1)}, bf16[192,1728]{1,0:T(8,128)(2,1)}, u32[]{:S(2)}, u32[]{:S(2)}) collective-permute-start(bf16[192,1728]{1,0:T(8,128)(2,1)} %collective-permute-done.6.refs_2_), channel_id=1, source_target_pairs={{0,16},{1,17},{2,18},{3,19},{4,20},{5,21},{6,22},{7,23},{8,24},{9,... | collective-permute-start | bytes 1990664 | tf_op jit(solution)/shard_map/ppermute | solution.py:247
  29.7 21.9 %collective-permute-start.1 = (bf16[96,1728]{1,0:T(8,128)(2,1)S(1)}, bf16[96,1728]{1,0:T(8,128)(2,1)S(1)}, u32[]{:S(2)}, u32[]{:S(2)}) collective-permute-start(bf16[96,1728]{1,0:T(8,128)(2,1)S(1)} %slice.16), channel_id=1, source_target_pairs={{0,48},{1,49},{2,50},{3,51},{4,52},{5,53},{6,54},{7,55},{8,56},{9,... | collective-permute-start | bytes 995336 | tf_op jit(solution)/shard_map/ppermute | solution.py:247
  31.2 24.4 %collective-permute-start.3 = (bf16[96,1728]{1,0:T(8,128)(2,1)S(1)}, bf16[96,1728]{1,0:T(8,128)(2,1)}, u32[]{:S(2)}, u32[]{:S(2)}) collective-permute-start(bf16[96,1728]{1,0:T(8,128)(2,1)S(1)} %slice.17), channel_id=1, source_target_pairs={{0,16},{1,17},{2,18},{3,19},{4,20},{5,21},{6,22},{7,23},{8,24},{9,... | collective-permute-start | bytes 995336 | tf_op jit(solution)/shard_map/ppermute | solution.py:247
  39.1 37.0 %all-to-all-start.2 = ((bf16[8,4,48,512]{3,2,1,0:T(8,128)(2,1)}), bf16[8,4,48,512]{3,2,1,0:T(8,128)(2,1)S(1)}, u32[]{:S(2)}, u32[]{:S(2)}) async-start(bf16[8,4,48,512]{3,2,1,0:T(8,128)(2,1)} %shard_map.71), calls=%async_computation.2 | async-start | bytes 3145728 | tf_op jit(solution)/shard_map/all_to_all | solution.py:282
  51.6 16.6 %copy-start.11 = (bf16[96,1728]{1,0:T(8,128)(2,1)}, bf16[96,1728]{1,0:T(8,128)(2,1)S(1)}, u32[]{:S(2)}) copy-start(bf16[96,1728]{1,0:T(8,128)(2,1)S(1)} %collective-permute-done.1.refs_0_) | copy-start | bytes 995332
  51.6 3.9 %collective-permute-start.4 = (bf16[96,1728]{1,0:T(8,128)(2,1)S(1)}, bf16[96,1728]{1,0:T(8,128)(2,1)S(1)}, u32[]{:S(2)}, u32[]{:S(2)}) collective-permute-start(bf16[96,1728]{1,0:T(8,128)(2,1)S(1)} %collective-permute-done.1.refs_0_), channel_id=1, source_target_pairs={{0,8},{1,9},{2,10},{3,11},{4,12},{5,13},{6,14},{7,15},{8,0},{9,1},... | collective-permute-start | bytes 995336 | tf_op jit(solution)/shard_map/ppermute | solution.py:247
  52.3 16.0 %copy-start.8 = (bf16[192,1728]{1,0:T(8,128)(2,1)}, bf16[192,1728]{1,0:T(8,128)(2,1)S(1)}, u32[]{:S(2)}) copy-start(bf16[192,1728]{1,0:T(8,128)(2,1)S(1)} %collective-permute-done.7.refs_4_) | copy-start | bytes 1990660
  52.4 9.8 %collective-permute-start.11 = (bf16[96,1728]{1,0:T(8,128)(2,1)S(1)}, bf16[96,1728]{1,0:T(8,128)(2,1)}, u32[]{:S(2)}, u32[]{:S(2)}) collective-permute-start(bf16[96,1728]{1,0:T(8,128)(2,1)S(1)} %slice.18), channel_id=1, source_target_pairs={{0,48},{1,49},{2,50},{3,51},{4,52},{5,53},{6,54},{7,55},{8,56},{9,... | collective-permute-start | bytes 995336 | tf_op jit(solution)/shard_map/ppermute | solution.py:247
  54.8 10.7 %collective-permute-start.12 = (bf16[96,1728]{1,0:T(8,128)(2,1)S(1)}, bf16[96,1728]{1,0:T(8,128)(2,1)}, u32[]{:S(2)}, u32[]{:S(2)}) collective-permute-start(bf16[96,1728]{1,0:T(8,128)(2,1)S(1)} %slice.19), channel_id=1, source_target_pairs={{0,16},{1,17},{2,18},{3,19},{4,20},{5,21},{6,22},{7,23},{8,24},{9,... | collective-permute-start | bytes 995336 | tf_op jit(solution)/shard_map/ppermute | solution.py:247
  55.0 13.3 %collective-permute-start.10 = (bf16[192,1728]{1,0:T(8,128)(2,1)}, bf16[192,1728]{1,0:T(8,128)(2,1)}, u32[]{:S(2)}, u32[]{:S(2)}) collective-permute-start(bf16[192,1728]{1,0:T(8,128)(2,1)} %collective-permute-done.9.refs_6_), channel_id=1, source_target_pairs={{0,8},{1,9},{2,10},{3,11},{4,12},{5,13},{6,14},{7,15},{8,0},{9,1},... | collective-permute-start | bytes 1990664 | tf_op jit(solution)/shard_map/ppermute | solution.py:247
  55.6 12.7 %collective-permute-start.8 = (bf16[192,1728]{1,0:T(8,128)(2,1)S(1)}, bf16[192,1728]{1,0:T(8,128)(2,1)}, u32[]{:S(2)}, u32[]{:S(2)}) collective-permute-start(bf16[192,1728]{1,0:T(8,128)(2,1)S(1)} %collective-permute-done.7.refs_4_), channel_id=1, source_target_pairs={{0,8},{1,9},{2,10},{3,11},{4,12},{5,13},{6,14},{7,15},{8,0},{9,1},... | collective-permute-start | bytes 1990664 | tf_op jit(solution)/shard_map/ppermute | solution.py:247
  55.6 12.7 %copy-start.12 = (bf16[96,1728]{1,0:T(8,128)(2,1)}, bf16[96,1728]{1,0:T(8,128)(2,1)S(1)}, u32[]{:S(2)}) copy-start(bf16[96,1728]{1,0:T(8,128)(2,1)S(1)} %collective-permute-done.4.refs_2_) | copy-start | bytes 995332
  55.6 12.4 %collective-permute-start.5 = (bf16[96,1728]{1,0:T(8,128)(2,1)}, bf16[96,1728]{1,0:T(8,128)(2,1)}, u32[]{:S(2)}, u32[]{:S(2)}) collective-permute-start(bf16[96,1728]{1,0:T(8,128)(2,1)} %collective-permute-done.3.refs_1_), channel_id=1, source_target_pairs={{0,8},{1,9},{2,10},{3,11},{4,12},{5,13},{6,14},{7,15},{8,0},{9,1},... | collective-permute-start | bytes 995336 | tf_op jit(solution)/shard_map/ppermute | solution.py:247
  62.2 5.8 %collective-permute-start.13 = (bf16[96,1728]{1,0:T(8,128)(2,1)}, bf16[96,1728]{1,0:T(8,128)(2,1)}, u32[]{:S(2)}, u32[]{:S(2)}) collective-permute-start(bf16[96,1728]{1,0:T(8,128)(2,1)} %collective-permute-done.11.refs_8_), channel_id=1, source_target_pairs={{0,8},{1,9},{2,10},{3,11},{4,12},{5,13},{6,14},{7,15},{8,0},{9,1},... | collective-permute-start | bytes 995336 | tf_op jit(solution)/shard_map/ppermute | solution.py:247
  65.5 2.7 %collective-permute-start.14 = (bf16[96,1728]{1,0:T(8,128)(2,1)}, bf16[96,1728]{1,0:T(8,128)(2,1)}, u32[]{:S(2)}, u32[]{:S(2)}) collective-permute-start(bf16[96,1728]{1,0:T(8,128)(2,1)} %collective-permute-done.12.refs_9_), channel_id=1, source_target_pairs={{0,8},{1,9},{2,10},{3,11},{4,12},{5,13},{6,14},{7,15},{8,0},{9,1},... | collective-permute-start | bytes 995336 | tf_op jit(solution)/shard_map/ppermute | solution.py:247
  76.1 26.3 %all-to-all-start = ((bf16[8,4,48,512]{3,2,1,0:T(8,128)(2,1)}), bf16[8,4,48,512]{3,2,1,0:T(8,128)(2,1)S(1)}, u32[]{:S(2)}, u32[]{:S(2)}) async-start(bf16[8,4,48,512]{3,2,1,0:T(8,128)(2,1)} %shard_map.68.refs_0_), calls=%async_computation | async-start | bytes 3145728 | tf_op jit(solution)/shard_map/all_to_all | solution.py:282
  81.0 1.4 copy-start.1
  82.6 1.2 copy-start.2
  102.4 24.9 %all-to-all-start.3 = ((bf16[8,4,48,512]{3,2,1,0:T(8,128)(2,1)}), bf16[8,4,48,512]{3,2,1,0:T(8,128)(2,1)S(1)}, u32[]{:S(2)}, u32[]{:S(2)}) async-start(bf16[8,4,48,512]{3,2,1,0:T(8,128)(2,1)} %copy-done.2), calls=%async_computation.3 | async-start | bytes 3145728 | tf_op jit(solution)/shard_map/all_to_all | solution.py:284
  107.4 24.8 %copy-start.9 = (s32[48,8]{0,1:T(8,128)S(1)}, s32[48,8]{0,1:T(8,128)}, u32[]{:S(2)}) copy-start(s32[48,8]{0,1:T(8,128)} %param.9) | copy-start | bytes 4612
  127.4 1.2 copy-start.5
  128.6 25.0 %all-to-all-start.1 = ((bf16[8,4,48,512]{3,2,1,0:T(8,128)(2,1)}), bf16[8,4,48,512]{3,2,1,0:T(8,128)(2,1)S(1)}, u32[]{:S(2)}, u32[]{:S(2)}) async-start(bf16[8,4,48,512]{3,2,1,0:T(8,128)(2,1)} %shard_map.69), calls=%async_computation.1 | async-start | bytes 3145728 | tf_op jit(solution)/shard_map/all_to_all | solution.py:284
  138.2 1.4 copy-start
  139.7 0.7 copy-start.3
  153.5 1.1 copy-start.4
  166.2 2.8 %collective-permute-start.19 = (bf16[8,24,1728]{2,1,0:T(8,128)(2,1)}, bf16[8,24,1728]{2,1,0:T(8,128)(2,1)S(1)}, u32[]{:S(2)}, u32[]{:S(2)}) collective-permute-start(bf16[8,24,1728]{2,1,0:T(8,128)(2,1)} %get-tuple-element.17), channel_id=1, source_target_pairs={{0,8},{1,9},{2,10},{3,11},{4,12},{5,13},{6,14},{7,15},{8,0},{9,1},... | collective-permute-start | bytes 1990664 | tf_op jit(solution)/shard_map/ppermute | solution.py:247
  171.1 17.0 %all-to-all-start.4 = ((bf16[8,24,1728]{2,1,0:T(8,128)(2,1)}), bf16[8,24,1728]{2,1,0:T(8,128)(2,1)S(1)}, u32[]{:S(2)}, u32[]{:S(2)}) async-start(bf16[8,24,1728]{2,1,0:T(8,128)(2,1)} %add_convert_fusion), calls=%async_computation.4 | async-start | bytes 1376256 | tf_op jit(solution)/shard_map/all_to_all | solution.py:292

commit v3 on v2

--- a/solution.py
+++ b/solution.py
@@ -15,9 +15,10 @@
 DP = ("zh", "x", "c")
 TENSOR = ("zl", "y")
 ANY = pl.BlockSpec(memory_space=pl.ANY)
-CHUNK_US = (4, 6)
 TILE = 896
 CHUNKS = (((0, 0), (1, 0), (0, 1), (0, 3)), ((0, 2), (1, 1), (1, 3), (1, 2)))
+CHUNK_US = (4, 6)
+MARK_US = 6
 
 
 def cosine_table():
@@ -37,7 +38,7 @@
 
 
 def output_kernel(pieces, info, ht_ref, target_ref, *refs):
-    blocks, (out_ref, w_ref, sems) = refs[:-3], refs[-3:]
+    blocks, (out_ref, w_ref, sems) = refs[: sum(pieces)], refs[-3:]
     core = info[0]
     shards, n, rows, _ = out_ref.shape
     half = shards * rows // 2
@@ -113,11 +114,44 @@
     )(parts, *after)
 
 
-def step_kernel(factor, info, ht_ref, rt_ref, m_ref, keep_ref, code_ref, *refs):
-    new_ref, mine_ref, other_ref = refs[-3:]
+def order_kernel(*refs):
+    pass
+
+
+def mark_kernel(*refs):
+    refs[-1][...] = jnp.zeros(refs[-1].shape, jnp.float32)
+
+
+def mark(arrays, us):
+    return pl.pallas_call(
+        mark_kernel,
+        out_shape=jax.ShapeDtypeStruct((8, 128), jnp.float32),
+        in_specs=[ANY] * len(arrays),
+        out_specs=pl.BlockSpec(memory_space=pltpu.VMEM),
+        cost_estimate=pl.CostEstimate(flops=int(us * 10**9), bytes_accessed=1, transcendentals=0),
+    )(*arrays)
+
+
+def in_order(array, before):
+    return pl.pallas_call(
+        order_kernel,
+        out_shape=jax.ShapeDtypeStruct(array.shape, array.dtype),
+        in_specs=[ANY, ANY],
+        out_specs=ANY,
+        input_output_aliases={0: 0},
+        cost_estimate=pl.CostEstimate(flops=1, bytes_accessed=1, transcendentals=0),
+    )(array, before)
+
+
+def step_kernel(factor, wants, info, ht_ref, rt_ref, m_ref, keep_ref, code_ref, *refs):
+    want_state, want_coeffs = wants
+    if want_coeffs:
+        mine_ref, other_ref = refs[-2:]
+        mine = mine_ref.shape[0]
+    if want_state:
+        new_ref = refs[-3 if want_coeffs else -1]
     rows = m_ref.shape[0]
     width = m_ref.shape[1]
-    mine = mine_ref.shape[0]
     rt = rt_ref[...].reshape(width, rt_ref.shape[2])
     keep = keep_ref[0]
     code = code_ref[0]
@@ -129,18 +163,19 @@
         )
         primed = DECAY * m_ref[f, :].astype(jnp.float32) + grad * factor
         low = primed.astype(jnp.bfloat16)
-        for a in range(0, width, 256):
+        for a in range(0, width if want_state else 0, 256):
             b = min(a + 256, width)
             gone = jnp.dot(low[:, a:b], keep[a:b, a:b], preferred_element_type=jnp.float32)
             new_ref[f, a:b] = (primed[:, a:b] - gone).astype(jnp.bfloat16)
-        coeffs = lax.dot_general(
-            code, low, (((1,), (1,)), ((), ())), preferred_element_type=jnp.float32
-        ).astype(jnp.bfloat16)
-        mine_ref[:, f] = coeffs[:mine]
-        other_ref[:, f] = coeffs[mine:]
-
-
-def momentum_step(chips, ht, rt, momentum, keep, code, state, factor):
+        if want_coeffs:
+            coeffs = lax.dot_general(
+                code, low, (((1,), (1,)), ((), ())), preferred_element_type=jnp.float32
+            ).astype(jnp.bfloat16)
+            mine_ref[:, f] = coeffs[:mine]
+            other_ref[:, f] = coeffs[mine:]
+
+
+def momentum_step(chips, ht, rt, momentum, keep, code, factor, wants, before):
     n = chips.shape[0]
     n_chips = code.shape[0]
     rows, width_all = momentum.shape
@@ -157,31 +192,26 @@
         pl.BlockSpec((1, kept, width), lambda u, c: (c[u], 0, 0)),
     ]
     args = [ht, rt, momentum, keep, code]
-    alias = {}
-    if state is not None:
-        in_specs += [ANY] * 3
-        args += state
-        alias = {6: 0, 7: 1, 8: 2}
-    return pl.pallas_call(
-        functools.partial(step_kernel, factor),
-        out_shape=(
-            jax.ShapeDtypeStruct((rows, width_all), jnp.bfloat16),
-            jax.ShapeDtypeStruct((n_chips, mine, rows), jnp.bfloat16),
-            jax.ShapeDtypeStruct((n_chips, mine, rows), jnp.bfloat16),
-        ),
+    alias = {6 + i: i for i in range(len(before))}
+    in_specs += [ANY] * len(before)
+    args += before
+    want_state, want_coeffs = wants
+    state_shape = jax.ShapeDtypeStruct((rows, width_all), jnp.bfloat16)
+    state_spec = pl.BlockSpec((rows, width), lambda u, c: (0, c[u]))
+    coeff_shape = jax.ShapeDtypeStruct((n_chips, mine, rows), jnp.bfloat16)
+    coeff_spec = pl.BlockSpec((None, mine, rows), lambda u, c: (c[u], 0, 0))
+    return pl.pallas_call(
+        functools.partial(step_kernel, factor, wants),
+        out_shape=(state_shape,) * want_state + (coeff_shape,) * (2 * want_coeffs),
         grid_spec=pltpu.PrefetchScalarGridSpec(
             num_scalar_prefetch=1,
             grid=(n,),
             in_specs=in_specs,
-            out_specs=(
-                pl.BlockSpec((rows, width), lambda u, c: (0, c[u])),
-                pl.BlockSpec((None, mine, rows), lambda u, c: (c[u], 0, 0)),
-                pl.BlockSpec((None, mine, rows), lambda u, c: (c[u], 0, 0)),
-            ),
+            out_specs=(state_spec,) * want_state + (coeff_spec,) * (2 * want_coeffs),
         ),
         input_output_aliases=alias,
         compiler_params=pltpu.CompilerParams(
-            vmem_limit_bytes=60 * 2**20, dimension_semantics=("arbitrary",)
+            vmem_limit_bytes=62 * 2**20, dimension_semantics=("arbitrary",)
         ),
         cost_estimate=pl.CostEstimate(
             flops=2 * n * rows * width * (tokens + 256 + kept),
@@ -269,24 +299,19 @@
     for chunk, us in zip(CHUNKS, CHUNK_US):
         at = jnp.stack([((zh + s[0]) % n_zh) * n_x + (x + s[1]) % n_x for s in chunk]).astype(jnp.int32)
         chips.append(at)
-        partials.append(
-            partial_output(
-                n_tensor,
-                jnp.concatenate([core, (at == shard).astype(jnp.int32)]),
-                ht,
-                target,
-                [b for s in chunk for b in (blocks[s], swapped[s])],
-                us,
-            )
-        )
-    received = [lax.all_to_all(p, TENSOR, 0, 0) for p in partials]
-    copies = [residual_copies(r, partials[i + 1 :]) for i, r in enumerate(received)]
-    gathered = [lax.all_to_all(k, TENSOR, 0, 0) for k in copies]
-
-    state = None
-    for at, whole in zip(chips, gathered):
-        state = momentum_step(at, ht, whole, momentum[0], keep, code, state, factor)
-    state, mine, other = state
+        info = jnp.concatenate([core, (at == shard).astype(jnp.int32)])
+        pairs = [b for s in chunk for b in (blocks[s], swapped[s])]
+        partials.append(partial_output(n_tensor, info, ht, target, pairs, us))
+    rest = [piece for s in CHUNKS[1] for piece in swapped[s]]
+    first = residual_copies(lax.all_to_all(partials[0], TENSOR, 0, 0), [mark(rest, MARK_US)])
+    first = lax.all_to_all(first, TENSOR, 0, 0)
+    last = residual_copies(lax.all_to_all(in_order(partials[1], first), TENSOR, 0, 0), [])
+    gathered = [first, lax.all_to_all(last, TENSOR, 0, 0)]
+
+    step = lambda k, *how: momentum_step(chips[k], ht, gathered[k], momentum[0], keep, code, factor, *how)
+    state, mine, other = step(0, (True, True), [])
+    mine, other = step(1, (False, True), [mine, other])
+    (state,) = step(1, (True, False), [state])
 
     pair = (mine.astype(jnp.float32) + send(other, c=1).astype(jnp.float32)).astype(jnp.bfloat16)
     total = jnp.sum(lax.all_to_all(pair, ("zh", "x"), 0, 0).astype(jnp.float32), axis=0)

time: 191 us -> 186 us (0.974)
  waiting for transfers between devices: 85.3 us -> 49.4 us
  blocking collectives: 0 us -> 23.8 us
  Pallas kernels: 45.7 us -> 56.5 us
  starting transfers between devices: 42.5 us -> 38.9 us
    all_to_all x4 -> x3, waiting for transfers between devices: 40.4 us -> 14.1 us  [the longest x1 12.4 us: per_device(): first = lax.all_to_all(first, TENSOR, 0, 0)]
    all_to_all x0 -> x1, blocking collectives: none -> 23.8 us  [per_device(): lax.all_to_all(in_order(partials[1], first), TENSOR, 0, 0)]
    all_to_all x1, waiting for transfers between devices: 13 us -> 2.48 us  [per_device(): lax.all_to_all(pair, ('zh', 'x'), 0, 0).astype(jnp.float32)]
    pallas_call x2 -> x5, Pallas kernels: 22.9 us -> 32.5 us  [the longest x3 31.9 us: momentum_step(): pl.pallas_call(functools.partial(step_kernel, factor, wants), out_shape=(...]
    all_to_all x4 -> x3, starting transfers between devices: 16.5 us -> 12.8 us  [the longest x1 4.64 us: per_device(): first = lax.all_to_all(first, TENSOR, 0, 0)]
    unnamed x27 -> x37, local copies, waits for them, and re-layouts: 7.16 us -> 6.75 us
  transfers between devices with their start and end apart: 25 -> 24, of which waited for: 11 -> 10; matrix products, arithmetic and copies ran while one was open for 2% -> 2% of each run, Pallas kernels for 18% -> 24%
where the time goes in v3:
time: 186 us; the launch traced here: 185 us
  Pallas kernels  56.5 us (30%)
  waiting for transfers between devices  49.4 us (27%)
  starting transfers between devices  38.9 us (21%)
  blocking collectives  23.8 us (13%)
  local copies, waits for them, and re-layouts  8.22 us (4%)
  other arithmetic  4.72 us (3%)
  matrix products  2.61 us (1%)
    ppermute x20, waiting for transfers between devices, per_device(): send = lambda v, **by: lax.ppermute(v, AXES, shift(sizes, **by))  32.8 us
    pallas_call x3, Pallas kernels, momentum_step(): pl.pallas_call(functools.partial(step_kernel, factor, wants), out_shape=(...  31.9 us
    all_to_all x1, blocking collectives, per_device(): lax.all_to_all(in_order(partials[1], first), TENSOR, 0, 0)  23.8 us
    ppermute x20, starting transfers between devices, per_device(): send = lambda v, **by: lax.ppermute(v, AXES, shift(sizes, **by))  22.5 us
    pallas_call x2, Pallas kernels, partial_output(): pl.pallas_call(functools.partial(output_kernel, pieces), out_shape=jax.Sh...  15.6 us
    all_to_all x1, waiting for transfers between devices, per_device(): first = lax.all_to_all(first, TENSOR, 0, 0)  12.4 us
    unnamed x37, local copies, waits for them, and re-layouts  6.75 us
    pallas_call x1, Pallas kernels, tables(): pl.pallas_call(table_kernel, out_shape=(jax.ShapeDtypeStruct((n_chips, pe...  5.56 us
  transfers between devices with their start and end apart: 24, of which 10 were waited for; matrix products, arithmetic and copies ran while one was open for 2% of the time, Pallas kernels for 24%

profile of v3, /device:TPU:1, one launch (start us, length us, event | category | flops | bytes accessed | tf_op | source)
XLA Modules:
  0.0 184.9 jit_solution(11655107965390704016)
XLA Ops:
  0.6 4.5 %collective-permute-start.6 = (bf16[192,1728]{1,0:T(8,128)(2,1)}, bf16[192,1728]{1,0:T(8,128)(2,1)}, u32[]{:S(2)}, u32[]{:S(2)}) collective-permute-start(bf16[192,1728]{1,0:T(8,128)(2,1)} %bitcast.39), channel_id=1, source_target_pairs={{0,64},{1,65},{2,66},{3,67},{4,68},{5,69},{6,70},{7,71},{8,72},{9,... | collective-permute-start | bytes 1990664 | tf_op jit(solution)/shard_map/ppermute | solution.py:277
  5.1 2.5 %collective-permute-start = (bf16[192,1728]{1,0:T(8,128)(2,1)}, bf16[192,1728]{1,0:T(8,128)(2,1)S(1)}, u32[]{:S(2)}, u32[]{:S(2)}) collective-permute-start(bf16[192,1728]{1,0:T(8,128)(2,1)} %bitcast.40), channel_id=1, source_target_pairs={{0,48},{1,49},{2,50},{3,51},{4,52},{5,53},{6,54},{7,55},{8,56},{9,... | collective-permute-start | bytes 1990664 | tf_op jit(solution)/shard_map/ppermute | solution.py:277
  7.6 1.2 collective-permute-start.15
  8.9 11.8 %collective-permute-done.6.refs_2_ = bf16[192,1728]{1,0:T(8,128)(2,1)} collective-permute-done((bf16[192,1728]{1,0:T(8,128)(2,1)}, bf16[192,1728]{1,0:T(8,128)(2,1)}, u32[]{:S(2)}, u32[]{:S(2)}) %collective-permute-start.6) | collective-permute-done | bytes 663584 | tf_op jit(solution)/shard_map/ppermute | solution.py:277
  20.6 1.2 collective-permute-start.16
  21.8 1.7 collective-permute-start.17
  23.6 1.1 collective-permute-done.2.refs_6_
  24.7 2.2 %collective-permute-start.18 = (bf16[192,1728]{1,0:T(8,128)(2,1)S(1)}, bf16[192,1728]{1,0:T(8,128)(2,1)}, u32[]{:S(2)}, u32[]{:S(2)}) collective-permute-start(bf16[192,1728]{1,0:T(8,128)(2,1)S(1)} %collective-permute-done.2.refs_6_), channel_id=1, source_target_pairs={{0,8},{1,9},{2,10},{3,11},{4,12},{5,13},{6,14},{7,15},{8,0},{9,1},... | collective-permute-start | bytes 1990664 | tf_op jit(solution)/shard_map/ppermute | solution.py:277
  26.9 0.1 collective-permute-start.7
  27.0 1.3 collective-permute-start.9
  28.4 0.6 compare_convert_fusion
  28.9 0.6 pad_add_fusion.3.info
  29.6 1.4 collective-permute-start.1
  31.0 0.1 collective-permute-start.3
  31.1 7.8 %shard_map.69 = bf16[8,4,48,512]{3,2,1,0:T(8,128)(2,1)} custom-call(s32[5]{0:T(128)} %pad_add_fusion.3.info, bf16[1728,512]{1,0:T(8,128)(2,1)} %bitcast.29, bf16[512,384]{1,0:T(8,128)(2,1)} %target_ref.3, bf16[192,1728]{1,0:T(8,128)(2,1)} %bitcast.43, bf16[192,1728]{1,0:T(8,128)(2,1)} %copy-done.9, bf16[192,1728]{1,0:T(8,128)(2,1)} %collective-permute-done.6.refs_2_, ...), custom_call_target="tpu_custom_call" | custom-call | flops 4000000000 | bytes 1 | tf_op jit(solution)/shard_map/pallas_call | solution.py:83
  38.9 4.5 %all-to-all-start = ((bf16[8,4,48,512]{3,2,1,0:T(8,128)(2,1)}), bf16[8,4,48,512]{3,2,1,0:T(8,128)(2,1)S(1)}, u32[]{:S(2)}, u32[]{:S(2)}) async-start(bf16[8,4,48,512]{3,2,1,0:T(8,128)(2,1)} %shard_map.69), calls=%async_computation | async-start | bytes 3145728 | tf_op jit(solution)/shard_map/all_to_all | solution.py:306
  43.4 8.2 %collective-permute-done.1.refs_0_ = bf16[96,1728]{1,0:T(8,128)(2,1)S(1)} collective-permute-done((bf16[96,1728]{1,0:T(8,128)(2,1)S(1)}, bf16[96,1728]{1,0:T(8,128)(2,1)S(1)}, u32[]{:S(2)}, u32[]{:S(2)}) %collective-permute-start.1) | collective-permute-done | bytes 331808 | tf_op jit(solution)/shard_map/ppermute | solution.py:277
  51.6 0.7 collective-permute-start.4
  52.4 1.4 collective-permute-start.11
  53.8 1.0 slice.19
  54.8 0.2 collective-permute-start.12
  55.0 0.6 collective-permute-start.10
  55.6 0.5 collective-permute-start.5
  56.1 6.0 %collective-permute-done.11.refs_8_ = bf16[96,1728]{1,0:T(8,128)(2,1)S(1)} collective-permute-done((bf16[96,1728]{1,0:T(8,128)(2,1)S(1)}, bf16[96,1728]{1,0:T(8,128)(2,1)S(1)}, u32[]{:S(2)}, u32[]{:S(2)}) %collective-permute-start.11) | collective-permute-done | bytes 331808 | tf_op jit(solution)/shard_map/ppermute | solution.py:277
  62.1 0.8 collective-permute-start.13
  62.9 2.5 %collective-permute-done.12.refs_9_ = bf16[96,1728]{1,0:T(8,128)(2,1)S(1)} collective-permute-done((bf16[96,1728]{1,0:T(8,128)(2,1)S(1)}, bf16[96,1728]{1,0:T(8,128)(2,1)S(1)}, u32[]{:S(2)}, u32[]{:S(2)}) %collective-permute-start.12) | collective-permute-done | bytes 331808 | tf_op jit(solution)/shard_map/ppermute | solution.py:277
  65.4 1.1 collective-permute-start.14
  66.6 1.3 collective-permute-done.14.refs_11_.refs_5_
  67.9 0.7 copy-done.17
  68.6 0.8 copy-done.10
  69.4 0.6 shard_map.70.refs_0_
  70.0 0.7 copy-done.2
  70.7 1.4 shard_map.71
  72.1 4.6 %all-to-all-start.1 = ((bf16[8,4,48,512]{3,2,1,0:T(8,128)(2,1)}), bf16[8,4,48,512]{3,2,1,0:T(8,128)(2,1)S(1)}, u32[]{:S(2)}, u32[]{:S(2)}) async-start(bf16[8,4,48,512]{3,2,1,0:T(8,128)(2,1)} %shard_map.71), calls=%async_computation.1 | async-start | bytes 3145728 | tf_op jit(solution)/shard_map/all_to_all | solution.py:307
  76.7 0.7 compare_convert_fusion.1
  77.4 0.6 pad_add_fusion.1.info
  78.0 7.8 %shard_map.68.refs_0_ = bf16[8,4,48,512]{3,2,1,0:T(8,128)(2,1)} custom-call(s32[5]{0:T(128)} %pad_add_fusion.1.info, bf16[1728,512]{1,0:T(8,128)(2,1)} %bitcast.30, bf16[512,384]{1,0:T(8,128)(2,1)} %target_ref.3, bf16[96,1728]{1,0:T(8,128)(2,1)} %copy-done.11, bf16[96,1728]{1,0:T(8,128)(2,1)} %collective-permute-done.3.refs_1_, bf16[96,1728]{1,0:T(8,128)(2,1)} %copy-done.12, ...), custom_call_target="tpu_custom_call" | custom-call | flops 6000000000 | bytes 1 | tf_op jit(solution)/shard_map/pallas_call | solution.py:83
  85.8 12.4 %all-to-all-done.1.refs_1_.rt_ref = bf16[8,4,48,512]{3,2,1,0:T(8,128)(2,1)S(1)} async-done(((bf16[8,4,48,512]{3,2,1,0:T(8,128)(2,1)}), bf16[8,4,48,512]{3,2,1,0:T(8,128)(2,1)S(1)}, u32[]{:S(2)}, u32[]{:S(2)}) %all-to-all-start.1) | async-done | bytes 1572896 | tf_op jit(solution)/shard_map/all_to_all | solution.py:307
  98.2 1.1 copy-done.4
  99.3 23.8 %all_to_all.25.parts_ref = bf16[8,4,48,512]{3,2,1,0:T(8,128)(2,1)S(1)} all-to-all(bf16[8,4,48,512]{3,2,1,0:T(8,128)(2,1)} %shard_map.72), channel_id=1, replica_groups=mesh['zh'=2,'x'=4,'c'=2,'zl'=2,'y'=4] {'zl','y'}, dimensions={0} | all-to-all | bytes 3145728 | tf_op jit(solution)/shard_map/all_to_all | solution.py:308
  123.1 1.4 shard_map.73
  124.5 3.7 %all-to-all-start.3 = ((bf16[8,4,48,512]{3,2,1,0:T(8,128)(2,1)}), bf16[8,4,48,512]{3,2,1,0:T(8,128)(2,1)S(1)}, u32[]{:S(2)}, u32[]{:S(2)}) async-start(bf16[8,4,48,512]{3,2,1,0:T(8,128)(2,1)} %shard_map.73), calls=%async_computation.3 | async-start | bytes 3145728 | tf_op jit(solution)/shard_map/all_to_all | solution.py:309
  128.2 0.1 copy.12
  128.3 0.1 reshape.33
  128.4 0.1 reshape.38.freqs_ref
  128.6 0.1 cosine_multiply_fusion.cosines_ref
  128.7 5.6 %shard_map.74 = (bf16[8,384,384]{2,1,0:T(8,128)(2,1)S(1)}, bf16[8,48,384]{2,1,0:T(8,128)(2,1)S(1)}) custom-call(s32[1]{0:T(128)} %bitcast.5.info, s32[8,48,1]{2,1,0:T(8,128)S(1)} %reshape.38.freqs_ref, f32[64,64]{1,0:T(8,128)S(1)} %cosine_multiply_fusion.cosines_ref), custom_call_target="tpu_custom_call" | custom-call | flops 1000000000 | bytes 4000000 | tf_op jit(solution)/shard_map/pallas_call | solution.py:255
  134.3 1.4 copy-done
  135.7 0.7 copy-done.1
  136.4 11.5 %shard_map.75 = (bf16[1728,3072]{1,0:T(8,128)(2,1)}, bf16[8,24,1728]{2,1,0:T(8,128)(2,1)}, bf16[8,24,1728]{2,1,0:T(8,128)(2,1)}) custom-call(s32[4]{0:T(128)} %get-tuple-element.17.info, bf16[1728,512]{1,0:T(8,128)(2,1)} %bitcast.31, bf16[8,4,48,512]{3,2,1,0:T(8,128)(2,1)} %copy-done.4, bf16[1728,3072]{1,0:T(8,128)(2,1)} %bitcast.26, ...), custom_call_target="tpu_custom_call" | custom-call | flops 4331667456 | bytes 12386304 | tf_op jit(solution)/shard_map/pallas_call | solution.py:203
  147.9 1.7 all-to-all-done.3.rt_ref
  149.6 1.1 copy-done.3
  150.7 9.7 %shard_map.77 = (bf16[8,24,1728]{2,1,0:T(8,128)(2,1)}, bf16[8,24,1728]{2,1,0:T(8,128)(2,1)}) custom-call(s32[4]{0:T(128)} %get-tuple-element.19.info, bf16[1728,512]{1,0:T(8,128)(2,1)} %bitcast.32, bf16[8,4,48,512]{3,2,1,0:T(8,128)(2,1)} %copy-done.3, bf16[1728,3072]{1,0:T(8,128)(2,1)} %bitcast.27, ...), custom_call_target="tpu_custom_call", output_to_operand_aliasing={{0}: (6, {}), {1}: (7, {})} | custom-call | flops 4331667456 | bytes 12386304 | tf_op jit(solution)/shard_map/pallas_call | solution.py:203
  160.4 0.9 collective-permute-start.19
  161.3 0.1 constant_dynamic-slice_fusion
  161.4 0.1 copy.14
  161.5 1.8 collective-permute-done.19
  163.3 2.1 %add_convert_fusion = bf16[8,24,1728]{2,1,0:T(8,128)(2,1)} fusion(bf16[8,24,1728]{2,1,0:T(8,128)(2,1)S(1)} %collective-permute-done.19, bf16[8,24,1728]{2,1,0:T(8,128)(2,1)} %get-tuple-element.14), kind=kLoop, calls=%fused_computation.1 | loop fusion | flops 1327104 | bytes 1990656 | tf_op jit(solution)/shard_map/convert_element_type | solution.py:316
  165.4 3.5 %all-to-all-start.4 = ((bf16[8,24,1728]{2,1,0:T(8,128)(2,1)}), bf16[8,24,1728]{2,1,0:T(8,128)(2,1)S(1)}, u32[]{:S(2)}, u32[]{:S(2)}) async-start(bf16[8,24,1728]{2,1,0:T(8,128)(2,1)} %add_convert_fusion), calls=%async_computation.4 | async-start | bytes 1376256 | tf_op jit(solution)/shard_map/all_to_all | solution.py:317
  168.9 0.3 convolution_multiply_fusion
  169.2 10.7 %shard_map.76 = bf16[1728,3072]{1,0:T(8,128)(2,1)} custom-call(s32[4]{0:T(128)} %get-tuple-element.19.info, bf16[1728,512]{1,0:T(8,128)(2,1)} %bitcast.33, bf16[8,4,48,512]{3,2,1,0:T(8,128)(2,1)} %copy-done.3, bf16[1728,3072]{1,0:T(8,128)(2,1)} %bitcast.28, bf16[8,384,384]{2,1,0:T(8,128)(2,1)} %copy-done, ...), custom_call_target="tpu_custom_call", output_to_operand_aliasing={{}: (6, {})} | custom-call | flops 4331667456 | bytes 12386304 | tf_op jit(solution)/shard_map/pallas_call | solution.py:203
  179.9 2.5 %all-to-all-done.4 = bf16[8,24,1728]{2,1,0:T(8,128)(2,1)S(1)} async-done(((bf16[8,24,1728]{2,1,0:T(8,128)(2,1)}), bf16[8,24,1728]{2,1,0:T(8,128)(2,1)S(1)}, u32[]{:S(2)}, u32[]{:S(2)}) %all-to-all-start.4) | async-done | bytes 663584 | tf_op jit(solution)/shard_map/all_to_all | solution.py:317
  182.4 0.1 convert_reduce_fusion
  182.5 2.3 %fusion = f32[3,64,1728]{2,1,0:T(8,128)} fusion(f32[3,8,64]{2,1,0:T(8,128)S(1)} %convolution_multiply_fusion, f32[24,1728]{1,0:T(8,128)S(1)} %convert_reduce_fusion), kind=kOutput, calls=%fused_computation.3 | convolution fusion | flops 31850496 | bytes 1499136 | tf_op jit(solution)/shard_map/ckf,ckj->cjf/dot_general | solution.py:323
  (52 shorter events, 0.2 us)
Async XLA Ops:
  0.6 20.0 %collective-permute-start.6 = (bf16[192,1728]{1,0:T(8,128)(2,1)}, bf16[192,1728]{1,0:T(8,128)(2,1)}, u32[]{:S(2)}, u32[]{:S(2)}) collective-permute-start(bf16[192,1728]{1,0:T(8,128)(2,1)} %bitcast.39), channel_id=1, source_target_pairs={{0,64},{1,65},{2,66},{3,67},{4,68},{5,69},{6,70},{7,71},{8,72},{9,... | collective-permute-start | bytes 1990664 | tf_op jit(solution)/shard_map/ppermute | solution.py:277
  5.1 16.7 %collective-permute-start = (bf16[192,1728]{1,0:T(8,128)(2,1)}, bf16[192,1728]{1,0:T(8,128)(2,1)S(1)}, u32[]{:S(2)}, u32[]{:S(2)}) collective-permute-start(bf16[192,1728]{1,0:T(8,128)(2,1)} %bitcast.40), channel_id=1, source_target_pairs={{0,48},{1,49},{2,50},{3,51},{4,52},{5,53},{6,54},{7,55},{8,56},{9,... | collective-permute-start | bytes 1990664 | tf_op jit(solution)/shard_map/ppermute | solution.py:277
  7.6 17.1 %collective-permute-start.2 = (bf16[192,1728]{1,0:T(8,128)(2,1)}, bf16[192,1728]{1,0:T(8,128)(2,1)S(1)}, u32[]{:S(2)}, u32[]{:S(2)}) collective-permute-start(bf16[192,1728]{1,0:T(8,128)(2,1)} %bitcast.41), channel_id=1, source_target_pairs={{0,16},{1,17},{2,18},{3,19},{4,20},{5,21},{6,22},{7,23},{8,24},{9,... | collective-permute-start | bytes 1990664 | tf_op jit(solution)/shard_map/ppermute | solution.py:277
  7.6 19.4 %collective-permute-start.15 = (bf16[192,1728]{1,0:T(8,128)(2,1)}, bf16[192,1728]{1,0:T(8,128)(2,1)S(1)}, u32[]{:S(2)}, u32[]{:S(2)}) collective-permute-start(bf16[192,1728]{1,0:T(8,128)(2,1)} %bitcast.42), channel_id=1, source_target_pairs={{0,8},{1,9},{2,10},{3,11},{4,12},{5,13},{6,14},{7,15},{8,0},{9,1},... | collective-permute-start | bytes 1990664 | tf_op jit(solution)/shard_map/ppermute | solution.py:277
  20.6 8.9 %collective-permute-start.16 = (bf16[192,1728]{1,0:T(8,128)(2,1)}, bf16[192,1728]{1,0:T(8,128)(2,1)}, u32[]{:S(2)}, u32[]{:S(2)}) collective-permute-start(bf16[192,1728]{1,0:T(8,128)(2,1)} %collective-permute-done.6.refs_2_), channel_id=1, source_target_pairs={{0,8},{1,9},{2,10},{3,11},{4,12},{5,13},{6,14},{7,15},{8,0},{9,1},... | collective-permute-start | bytes 1990664 | tf_op jit(solution)/shard_map/ppermute | solution.py:277
  21.8 9.3 %copy-start.5 = (bf16[192,1728]{1,0:T(8,128)(2,1)}, bf16[192,1728]{1,0:T(8,128)(2,1)S(1)}, u32[]{:S(2)}) copy-start(bf16[192,1728]{1,0:T(8,128)(2,1)S(1)} %collective-permute-done.refs_4_) | copy-start | bytes 1990660
  21.8 9.1 %collective-permute-start.17 = (bf16[192,1728]{1,0:T(8,128)(2,1)S(1)}, bf16[192,1728]{1,0:T(8,128)(2,1)}, u32[]{:S(2)}, u32[]{:S(2)}) collective-permute-start(bf16[192,1728]{1,0:T(8,128)(2,1)S(1)} %collective-permute-done.refs_4_), channel_id=1, source_target_pairs={{0,8},{1,9},{2,10},{3,11},{4,12},{5,13},{6,14},{7,15},{8,0},{9,1},... | collective-permute-start | bytes 1990664 | tf_op jit(solution)/shard_map/ppermute | solution.py:277
  24.7 6.4 %copy-start.6 = (bf16[192,1728]{1,0:T(8,128)(2,1)}, bf16[192,1728]{1,0:T(8,128)(2,1)S(1)}, u32[]{:S(2)}) copy-start(bf16[192,1728]{1,0:T(8,128)(2,1)S(1)} %collective-permute-done.2.refs_6_) | copy-start | bytes 1990660
  24.7 6.4 %collective-permute-start.18 = (bf16[192,1728]{1,0:T(8,128)(2,1)S(1)}, bf16[192,1728]{1,0:T(8,128)(2,1)}, u32[]{:S(2)}, u32[]{:S(2)}) collective-permute-start(bf16[192,1728]{1,0:T(8,128)(2,1)S(1)} %collective-permute-done.2.refs_6_), channel_id=1, source_target_pairs={{0,8},{1,9},{2,10},{3,11},{4,12},{5,13},{6,14},{7,15},{8,0},{9,1},... | collective-permute-start | bytes 1990664 | tf_op jit(solution)/shard_map/ppermute | solution.py:277
  26.9 25.4 %collective-permute-start.7 = (bf16[192,1728]{1,0:T(8,128)(2,1)}, bf16[192,1728]{1,0:T(8,128)(2,1)S(1)}, u32[]{:S(2)}, u32[]{:S(2)}) collective-permute-start(bf16[192,1728]{1,0:T(8,128)(2,1)} %collective-permute-done.6.refs_2_), channel_id=1, source_target_pairs={{0,48},{1,49},{2,50},{3,51},{4,52},{5,53},{6,54},{7,55},{8,56},{9,... | collective-permute-start | bytes 1990664 | tf_op jit(solution)/shard_map/ppermute | solution.py:277
  27.0 1.3 copy-start.9
  27.0 26.7 %collective-permute-start.9 = (bf16[192,1728]{1,0:T(8,128)(2,1)}, bf16[192,1728]{1,0:T(8,128)(2,1)}, u32[]{:S(2)}, u32[]{:S(2)}) collective-permute-start(bf16[192,1728]{1,0:T(8,128)(2,1)} %collective-permute-done.6.refs_2_), channel_id=1, source_target_pairs={{0,16},{1,17},{2,18},{3,19},{4,20},{5,21},{6,22},{7,23},{8,24},{9,... | collective-permute-start | bytes 1990664 | tf_op jit(solution)/shard_map/ppermute | solution.py:277
  29.6 22.1 %collective-permute-start.1 = (bf16[96,1728]{1,0:T(8,128)(2,1)S(1)}, bf16[96,1728]{1,0:T(8,128)(2,1)S(1)}, u32[]{:S(2)}, u32[]{:S(2)}) collective-permute-start(bf16[96,1728]{1,0:T(8,128)(2,1)S(1)} %slice.16), channel_id=1, source_target_pairs={{0,48},{1,49},{2,50},{3,51},{4,52},{5,53},{6,54},{7,55},{8,56},{9,... | collective-permute-start | bytes 995336 | tf_op jit(solution)/shard_map/ppermute | solution.py:277
  31.0 24.6 %collective-permute-start.3 = (bf16[96,1728]{1,0:T(8,128)(2,1)S(1)}, bf16[96,1728]{1,0:T(8,128)(2,1)}, u32[]{:S(2)}, u32[]{:S(2)}) collective-permute-start(bf16[96,1728]{1,0:T(8,128)(2,1)S(1)} %slice.17), channel_id=1, source_target_pairs={{0,16},{1,17},{2,18},{3,19},{4,20},{5,21},{6,22},{7,23},{8,24},{9,... | collective-permute-start | bytes 995336 | tf_op jit(solution)/shard_map/ppermute | solution.py:277
  38.9 31.1 %all-to-all-start = ((bf16[8,4,48,512]{3,2,1,0:T(8,128)(2,1)}), bf16[8,4,48,512]{3,2,1,0:T(8,128)(2,1)S(1)}, u32[]{:S(2)}, u32[]{:S(2)}) async-start(bf16[8,4,48,512]{3,2,1,0:T(8,128)(2,1)} %shard_map.69), calls=%async_computation | async-start | bytes 3145728 | tf_op jit(solution)/shard_map/all_to_all | solution.py:306
  51.6 18.4 %copy-start.11 = (bf16[96,1728]{1,0:T(8,128)(2,1)}, bf16[96,1728]{1,0:T(8,128)(2,1)S(1)}, u32[]{:S(2)}) copy-start(bf16[96,1728]{1,0:T(8,128)(2,1)S(1)} %collective-permute-done.1.refs_0_) | copy-start | bytes 995332
  51.6 3.9 %collective-permute-start.4 = (bf16[96,1728]{1,0:T(8,128)(2,1)S(1)}, bf16[96,1728]{1,0:T(8,128)(2,1)S(1)}, u32[]{:S(2)}, u32[]{:S(2)}) collective-permute-start(bf16[96,1728]{1,0:T(8,128)(2,1)S(1)} %collective-permute-done.1.refs_0_), channel_id=1, source_target_pairs={{0,8},{1,9},{2,10},{3,11},{4,12},{5,13},{6,14},{7,15},{8,0},{9,1},... | collective-permute-start | bytes 995336 | tf_op jit(solution)/shard_map/ppermute | solution.py:277
  52.3 17.7 %copy-start.7 = (bf16[192,1728]{1,0:T(8,128)(2,1)}, bf16[192,1728]{1,0:T(8,128)(2,1)S(1)}, u32[]{:S(2)}) copy-start(bf16[192,1728]{1,0:T(8,128)(2,1)S(1)} %collective-permute-done.7.refs_4_) | copy-start | bytes 1990660
  52.4 9.7 %collective-permute-start.11 = (bf16[96,1728]{1,0:T(8,128)(2,1)S(1)}, bf16[96,1728]{1,0:T(8,128)(2,1)S(1)}, u32[]{:S(2)}, u32[]{:S(2)}) collective-permute-start(bf16[96,1728]{1,0:T(8,128)(2,1)S(1)} %slice.18), channel_id=1, source_target_pairs={{0,48},{1,49},{2,50},{3,51},{4,52},{5,53},{6,54},{7,55},{8,56},{9,... | collective-permute-start | bytes 995336 | tf_op jit(solution)/shard_map/ppermute | solution.py:277
  54.8 10.6 %collective-permute-start.12 = (bf16[96,1728]{1,0:T(8,128)(2,1)S(1)}, bf16[96,1728]{1,0:T(8,128)(2,1)S(1)}, u32[]{:S(2)}, u32[]{:S(2)}) collective-permute-start(bf16[96,1728]{1,0:T(8,128)(2,1)S(1)} %slice.19), channel_id=1, source_target_pairs={{0,16},{1,17},{2,18},{3,19},{4,20},{5,21},{6,22},{7,23},{8,24},{9,... | collective-permute-start | bytes 995336 | tf_op jit(solution)/shard_map/ppermute | solution.py:277
  55.0 12.9 %collective-permute-start.10 = (bf16[192,1728]{1,0:T(8,128)(2,1)}, bf16[192,1728]{1,0:T(8,128)(2,1)}, u32[]{:S(2)}, u32[]{:S(2)}) collective-permute-start(bf16[192,1728]{1,0:T(8,128)(2,1)} %collective-permute-done.9.refs_6_), channel_id=1, source_target_pairs={{0,8},{1,9},{2,10},{3,11},{4,12},{5,13},{6,14},{7,15},{8,0},{9,1},... | collective-permute-start | bytes 1990664 | tf_op jit(solution)/shard_map/ppermute | solution.py:277
  55.6 13.0 %collective-permute-start.8 = (bf16[192,1728]{1,0:T(8,128)(2,1)S(1)}, bf16[192,1728]{1,0:T(8,128)(2,1)S(1)}, u32[]{:S(2)}, u32[]{:S(2)}) collective-permute-start(bf16[192,1728]{1,0:T(8,128)(2,1)S(1)} %collective-permute-done.7.refs_4_), channel_id=1, source_target_pairs={{0,8},{1,9},{2,10},{3,11},{4,12},{5,13},{6,14},{7,15},{8,0},{9,1},... | collective-permute-start | bytes 1990664 | tf_op jit(solution)/shard_map/ppermute | solution.py:277
  55.6 12.3 %copy-start.12 = (bf16[96,1728]{1,0:T(8,128)(2,1)}, bf16[96,1728]{1,0:T(8,128)(2,1)S(1)}, u32[]{:S(2)}) copy-start(bf16[96,1728]{1,0:T(8,128)(2,1)S(1)} %collective-permute-done.4.refs_2_.refs_0_) | copy-start | bytes 995332
  55.6 11.0 %collective-permute-start.5 = (bf16[96,1728]{1,0:T(8,128)(2,1)}, bf16[96,1728]{1,0:T(8,128)(2,1)S(1)}, u32[]{:S(2)}, u32[]{:S(2)}) collective-permute-start(bf16[96,1728]{1,0:T(8,128)(2,1)} %collective-permute-done.3.refs_1_), channel_id=1, source_target_pairs={{0,8},{1,9},{2,10},{3,11},{4,12},{5,13},{6,14},{7,15},{8,0},{9,1},... | collective-permute-start | bytes 995336 | tf_op jit(solution)/shard_map/ppermute | solution.py:277
  62.1 5.7 %copy-start.13 = (bf16[96,1728]{1,0:T(8,128)(2,1)}, bf16[96,1728]{1,0:T(8,128)(2,1)S(1)}, u32[]{:S(2)}) copy-start(bf16[96,1728]{1,0:T(8,128)(2,1)S(1)} %collective-permute-done.11.refs_8_) | copy-start | bytes 995332
  62.1 4.4 %collective-permute-start.13 = (bf16[96,1728]{1,0:T(8,128)(2,1)S(1)}, bf16[96,1728]{1,0:T(8,128)(2,1)S(1)}, u32[]{:S(2)}, u32[]{:S(2)}) collective-permute-start(bf16[96,1728]{1,0:T(8,128)(2,1)S(1)} %collective-permute-done.11.refs_8_), channel_id=1, source_target_pairs={{0,8},{1,9},{2,10},{3,11},{4,12},{5,13},{6,14},{7,15},{8,0},{9,1},... | collective-permute-start | bytes 995336 | tf_op jit(solution)/shard_map/ppermute | solution.py:277
  65.4 2.4 %copy-start.14 = (bf16[96,1728]{1,0:T(8,128)(2,1)}, bf16[96,1728]{1,0:T(8,128)(2,1)S(1)}, u32[]{:S(2)}) copy-start(bf16[96,1728]{1,0:T(8,128)(2,1)S(1)} %collective-permute-done.12.refs_9_) | copy-start | bytes 995332
  65.4 2.4 %collective-permute-start.14 = (bf16[96,1728]{1,0:T(8,128)(2,1)S(1)}, bf16[96,1728]{1,0:T(8,128)(2,1)S(1)}, u32[]{:S(2)}, u32[]{:S(2)}) collective-permute-start(bf16[96,1728]{1,0:T(8,128)(2,1)S(1)} %collective-permute-done.12.refs_9_), channel_id=1, source_target_pairs={{0,8},{1,9},{2,10},{3,11},{4,12},{5,13},{6,14},{7,15},{8,0},{9,1},... | collective-permute-start | bytes 995336 | tf_op jit(solution)/shard_map/ppermute | solution.py:277
  66.5 1.3 copy-start.15
  66.6 1.3 copy-start.16
  67.8 0.7 copy-start.17
  68.6 0.8 copy-start.10
  70.0 0.7 copy-start.2
  72.1 26.1 %all-to-all-start.1 = ((bf16[8,4,48,512]{3,2,1,0:T(8,128)(2,1)}), bf16[8,4,48,512]{3,2,1,0:T(8,128)(2,1)S(1)}, u32[]{:S(2)}, u32[]{:S(2)}) async-start(bf16[8,4,48,512]{3,2,1,0:T(8,128)(2,1)} %shard_map.71), calls=%async_computation.1 | async-start | bytes 3145728 | tf_op jit(solution)/shard_map/all_to_all | solution.py:307
  98.2 1.1 copy-start.4
  124.5 3.7 %copy-start.8 = (s32[48,8]{0,1:T(8,128)S(1)}, s32[48,8]{0,1:T(8,128)}, u32[]{:S(2)}) copy-start(s32[48,8]{0,1:T(8,128)} %param.9) | copy-start | bytes 4612
  124.5 25.1 %all-to-all-start.3 = ((bf16[8,4,48,512]{3,2,1,0:T(8,128)(2,1)}), bf16[8,4,48,512]{3,2,1,0:T(8,128)(2,1)S(1)}, u32[]{:S(2)}, u32[]{:S(2)}) async-start(bf16[8,4,48,512]{3,2,1,0:T(8,128)(2,1)} %shard_map.73), calls=%async_computation.3 | async-start | bytes 3145728 | tf_op jit(solution)/shard_map/all_to_all | solution.py:309
  134.3 1.4 copy-start
  135.7 0.7 copy-start.1
  149.6 1.1 copy-start.3
  160.4 2.8 %collective-permute-start.19 = (bf16[8,24,1728]{2,1,0:T(8,128)(2,1)}, bf16[8,24,1728]{2,1,0:T(8,128)(2,1)S(1)}, u32[]{:S(2)}, u32[]{:S(2)}) collective-permute-start(bf16[8,24,1728]{2,1,0:T(8,128)(2,1)} %get-tuple-element.15), channel_id=1, source_target_pairs={{0,8},{1,9},{2,10},{3,11},{4,12},{5,13},{6,14},{7,15},{8,0},{9,1},... | collective-permute-start | bytes 1990664 | tf_op jit(solution)/shard_map/ppermute | solution.py:277
  165.4 17.0 %all-to-all-start.4 = ((bf16[8,24,1728]{2,1,0:T(8,128)(2,1)}), bf16[8,24,1728]{2,1,0:T(8,128)(2,1)S(1)}, u32[]{:S(2)}, u32[]{:S(2)}) async-start(bf16[8,24,1728]{2,1,0:T(8,128)(2,1)} %add_convert_fusion), calls=%async_computation.4 | async-start | bytes 1376256 | tf_op jit(solution)/shard_map/all_to_all | solution.py:317

commit v4 on v3

--- a/solution.py
+++ b/solution.py
@@ -286,11 +286,11 @@
 
     cut = own.shape[0] // 2
     blocks = {(0, 0): [own], (1, 0): [send(own, zh=1)], (0, 1): [send(own, x=-1)], (0, 3): [send(own, x=1)]}
-    for z in range(2):
-        if z:
-            blocks[z, 1] = [send(blocks[z, 0][0], x=-1)]
-            blocks[z, 3] = [send(blocks[z, 0][0], x=1)]
-        blocks[z, 2] = [send(blocks[z, 1][0][:cut], x=-1), send(blocks[z, 3][0][cut:], x=1)]
+    blocks[0, 2] = [send(blocks[0, 1][0][:cut], x=-1), send(blocks[0, 3][0][cut:], x=1)]
+    halves = (blocks[1, 0][0][:cut], blocks[1, 0][0][cut:])
+    blocks[1, 1] = [send(h, x=-1) for h in halves]
+    blocks[1, 3] = [send(h, x=1) for h in halves]
+    blocks[1, 2] = [send(blocks[1, 1][0], x=-1), send(blocks[1, 3][1], x=1)]
     swapped = {s: [send(piece, c=1) for piece in b] for s, b in blocks.items()}
     keep, code = tables(freqs, c, n_chips)
 

time: 186 us -> 191 us (1.027)
  starting transfers between devices: 38.9 us -> 50.6 us
  waiting for transfers between devices: 49.4 us -> 43.1 us
    ppermute x20 -> x24, starting transfers between devices: 22.5 us -> 33.3 us  [per_device(): send = lambda v, **by: lax.ppermute(v, AXES, shift(sizes, **by))]
    ppermute x20 -> x24, waiting for transfers between devices: 32.8 us -> 24 us  [per_device(): send = lambda v, **by: lax.ppermute(v, AXES, shift(sizes, **by))]
    all_to_all x1, waiting for transfers between devices: 0.01 us -> 2.68 us  [per_device(): lax.all_to_all(partials[0], TENSOR, 0, 0)]
    all_to_all x1, starting transfers between devices: 3.54 us -> 5.52 us  [per_device(): lax.all_to_all(pair, ('zh', 'x'), 0, 0).astype(jnp.float32)]
  transfers between devices with their start and end apart: 24 -> 28, of which waited for: 10 -> 13; matrix products, arithmetic and copies ran while one was open for 2% -> 2% of each run, Pallas kernels for 24% -> 23%
where the time goes in v4:
time: 191 us; the launch traced here: 190 us
  Pallas kernels  56.5 us (30%)
  starting transfers between devices  50.6 us (26%)
  waiting for transfers between devices  43.1 us (23%)
  blocking collectives  24 us (13%)
  local copies, waits for them, and re-layouts  7.35 us (4%)
  other arithmetic  4.89 us (3%)
  matrix products  2.61 us (1%)
    ppermute x24, starting transfers between devices, per_device(): send = lambda v, **by: lax.ppermute(v, AXES, shift(sizes, **by))  33.3 us
    pallas_call x3, Pallas kernels, momentum_step(): pl.pallas_call(functools.partial(step_kernel, factor, wants), out_shape=(...  31.9 us
    ppermute x24, waiting for transfers between devices, per_device(): send = lambda v, **by: lax.ppermute(v, AXES, shift(sizes, **by))  24 us
    all_to_all x1, blocking collectives, per_device(): lax.all_to_all(in_order(partials[1], first), TENSOR, 0, 0)  24 us
    pallas_call x2, Pallas kernels, partial_output(): pl.pallas_call(functools.partial(output_kernel, pieces), out_shape=jax.Sh...  15.7 us
    all_to_all x1, waiting for transfers between devices, per_device(): first = lax.all_to_all(first, TENSOR, 0, 0)  12.2 us
    unnamed x37, local copies, waits for them, and re-layouts  5.89 us
    pallas_call x1, Pallas kernels, tables(): pl.pallas_call(table_kernel, out_shape=(jax.ShapeDtypeStruct((n_chips, pe...  5.56 us
  transfers between devices with their start and end apart: 28, of which 13 were waited for; matrix products, arithmetic and copies ran while one was open for 2% of the time, Pallas kernels for 23%

profile of v4, /device:TPU:1, one launch (start us, length us, event | category | flops | bytes accessed | tf_op | source)
XLA Modules:
  0.0 190.0 jit_solution(8427640028382004107)
XLA Ops:
  0.6 4.5 %collective-permute-start.6 = (bf16[192,1728]{1,0:T(8,128)(2,1)}, bf16[192,1728]{1,0:T(8,128)(2,1)S(1)}, u32[]{:S(2)}, u32[]{:S(2)}) collective-permute-start(bf16[192,1728]{1,0:T(8,128)(2,1)} %bitcast.39), channel_id=1, source_target_pairs={{0,64},{1,65},{2,66},{3,67},{4,68},{5,69},{6,70},{7,71},{8,72},{9,... | collective-permute-start | bytes 1990664 | tf_op jit(solution)/shard_map/ppermute | solution.py:277
  5.1 2.5 %collective-permute-start = (bf16[192,1728]{1,0:T(8,128)(2,1)}, bf16[192,1728]{1,0:T(8,128)(2,1)S(1)}, u32[]{:S(2)}, u32[]{:S(2)}) collective-permute-start(bf16[192,1728]{1,0:T(8,128)(2,1)} %bitcast.40), channel_id=1, source_target_pairs={{0,48},{1,49},{2,50},{3,51},{4,52},{5,53},{6,54},{7,55},{8,56},{9,... | collective-permute-start | bytes 1990664 | tf_op jit(solution)/shard_map/ppermute | solution.py:277
  7.6 1.2 collective-permute-start.19
  8.9 11.7 %collective-permute-done.6.refs_2_ = bf16[192,1728]{1,0:T(8,128)(2,1)S(1)} collective-permute-done((bf16[192,1728]{1,0:T(8,128)(2,1)}, bf16[192,1728]{1,0:T(8,128)(2,1)S(1)}, u32[]{:S(2)}, u32[]{:S(2)}) %collective-permute-start.6) | collective-permute-done | bytes 663584 | tf_op jit(solution)/shard_map/ppermute | solution.py:277
  20.5 1.2 collective-permute-start.20
  21.7 1.8 collective-permute-start.21
  23.6 1.2 collective-permute-done.2.refs_6_
  24.8 2.2 %collective-permute-start.22 = (bf16[192,1728]{1,0:T(8,128)(2,1)}, bf16[192,1728]{1,0:T(8,128)(2,1)}, u32[]{:S(2)}, u32[]{:S(2)}) collective-permute-start(bf16[192,1728]{1,0:T(8,128)(2,1)} %collective-permute-done.2.refs_6_), channel_id=1, source_target_pairs={{0,8},{1,9},{2,10},{3,11},{4,12},{5,13},{6,14},{7,15},{8,0},{9,1},... | collective-permute-start | bytes 1990664 | tf_op jit(solution)/shard_map/ppermute | solution.py:277
  27.2 0.6 compare_convert_fusion
  27.8 0.6 pad_add_fusion.3.info
  28.5 1.0 slice.17
  29.5 1.5 collective-permute-start.12
  31.0 6.0 %collective-permute-done.7.refs_4_ = bf16[96,1728]{1,0:T(8,128)(2,1)S(1)} collective-permute-done((bf16[96,1728]{1,0:T(8,128)(2,1)S(1)}, bf16[96,1728]{1,0:T(8,128)(2,1)S(1)}, u32[]{:S(2)}, u32[]{:S(2)}) %collective-permute-start.7) | collective-permute-done | bytes 331808 | tf_op jit(solution)/shard_map/ppermute | solution.py:277
  36.9 0.7 collective-permute-start.8
  37.6 0.8 collective-permute-start.11
  38.4 1.9 collective-permute-start.1
  40.3 7.8 %shard_map.69 = bf16[8,4,48,512]{3,2,1,0:T(8,128)(2,1)} custom-call(s32[5]{0:T(128)} %pad_add_fusion.3.info, bf16[1728,512]{1,0:T(8,128)(2,1)} %bitcast.29, bf16[512,384]{1,0:T(8,128)(2,1)} %target_ref.3, bf16[192,1728]{1,0:T(8,128)(2,1)} %bitcast.43, bf16[192,1728]{1,0:T(8,128)(2,1)} %collective-permute-done.19.refs_1_, bf16[192,1728]{1,0:T(8,128)(2,1)} %copy-done.5, ...), custom_call_target="tpu_custom_call" | custom-call | flops 4000000000 | bytes 1 | tf_op jit(solution)/shard_map/pallas_call | solution.py:83
  48.1 4.5 %all-to-all-start = ((bf16[8,4,48,512]{3,2,1,0:T(8,128)(2,1)}), bf16[8,4,48,512]{3,2,1,0:T(8,128)(2,1)S(1)}, u32[]{:S(2)}, u32[]{:S(2)}) async-start(bf16[8,4,48,512]{3,2,1,0:T(8,128)(2,1)} %shard_map.69), calls=%async_computation | async-start | bytes 3145728 | tf_op jit(solution)/shard_map/all_to_all | solution.py:306
  52.6 2.7 %collective-permute-start.15 = (bf16[96,1728]{1,0:T(8,128)(2,1)S(1)}, bf16[96,1728]{1,0:T(8,128)(2,1)S(1)}, u32[]{:S(2)}, u32[]{:S(2)}) collective-permute-start(bf16[96,1728]{1,0:T(8,128)(2,1)S(1)} %collective-permute-done.7.refs_4_), channel_id=1, source_target_pairs={{0,48},{1,49},{2,50},{3,51},{4,52},{5,53},{6,54},{7,55},{8,56},{9,... | collective-permute-start | bytes 995336 | tf_op jit(solution)/shard_map/ppermute | solution.py:277
  55.3 3.0 %collective-permute-start.14 = (bf16[96,1728]{1,0:T(8,128)(2,1)}, bf16[96,1728]{1,0:T(8,128)(2,1)S(1)}, u32[]{:S(2)}, u32[]{:S(2)}) collective-permute-start(bf16[96,1728]{1,0:T(8,128)(2,1)} %collective-permute-done.12.refs_9_), channel_id=1, source_target_pairs={{0,8},{1,9},{2,10},{3,11},{4,12},{5,13},{6,14},{7,15},{8,0},{9,1},... | collective-permute-start | bytes 995336 | tf_op jit(solution)/shard_map/ppermute | solution.py:277
  58.3 0.1 collective-permute-start.9
  58.4 0.4 collective-permute-start.10
  58.8 1.2 collective-permute-done.15.refs_12_
  60.0 3.6 %collective-permute-start.13 = (bf16[96,1728]{1,0:T(8,128)(2,1)}, bf16[96,1728]{1,0:T(8,128)(2,1)S(1)}, u32[]{:S(2)}, u32[]{:S(2)}) collective-permute-start(bf16[96,1728]{1,0:T(8,128)(2,1)} %collective-permute-done.11.refs_8_), channel_id=1, source_target_pairs={{0,8},{1,9},{2,10},{3,11},{4,12},{5,13},{6,14},{7,15},{8,0},{9,1},... | collective-permute-start | bytes 995336 | tf_op jit(solution)/shard_map/ppermute | solution.py:277
  63.6 3.6 %collective-permute-start.4 = (bf16[96,1728]{1,0:T(8,128)(2,1)}, bf16[96,1728]{1,0:T(8,128)(2,1)S(1)}, u32[]{:S(2)}, u32[]{:S(2)}) collective-permute-start(bf16[96,1728]{1,0:T(8,128)(2,1)} %collective-permute-done.1.refs_0_), channel_id=1, source_target_pairs={{0,8},{1,9},{2,10},{3,11},{4,12},{5,13},{6,14},{7,15},{8,0},{9,1},... | collective-permute-start | bytes 995336 | tf_op jit(solution)/shard_map/ppermute | solution.py:277
  67.2 0.1 collective-permute-start.5
  67.3 0.5 collective-permute-start.17
  67.8 0.1 collective-permute-start.18
  67.9 0.8 collective-permute-done.4.refs_2_.refs_0_
  68.7 0.5 collective-permute-done.5.refs_3_.refs_1_
  69.2 0.8 collective-permute-done.17.refs_14_.refs_6_
  70.0 0.1 collective-permute-done.18.refs_15_.refs_7_
  70.1 0.6 copy-done.17
  70.7 0.6 shard_map.70.refs_0_
  71.3 2.7 %all-to-all-done.parts_ref = bf16[8,4,48,512]{3,2,1,0:T(8,128)(2,1)S(1)} async-done(((bf16[8,4,48,512]{3,2,1,0:T(8,128)(2,1)}), bf16[8,4,48,512]{3,2,1,0:T(8,128)(2,1)S(1)}, u32[]{:S(2)}, u32[]{:S(2)}) %all-to-all-start) | async-done | bytes 1572896 | tf_op jit(solution)/shard_map/all_to_all | solution.py:306
  74.0 0.7 copy-done.2
  74.7 1.4 shard_map.71
  76.0 3.6 %all-to-all-start.1 = ((bf16[8,4,48,512]{3,2,1,0:T(8,128)(2,1)}), bf16[8,4,48,512]{3,2,1,0:T(8,128)(2,1)S(1)}, u32[]{:S(2)}, u32[]{:S(2)}) async-start(bf16[8,4,48,512]{3,2,1,0:T(8,128)(2,1)} %shard_map.71), calls=%async_computation.1 | async-start | bytes 3145728 | tf_op jit(solution)/shard_map/all_to_all | solution.py:307
  79.7 0.7 compare_convert_fusion.1
  80.3 0.6 pad_add_fusion.1.info
  80.9 7.9 %shard_map.68.refs_0_ = bf16[8,4,48,512]{3,2,1,0:T(8,128)(2,1)} custom-call(s32[5]{0:T(128)} %pad_add_fusion.1.info, bf16[1728,512]{1,0:T(8,128)(2,1)} %bitcast.30, bf16[512,384]{1,0:T(8,128)(2,1)} %target_ref.3, bf16[96,1728]{1,0:T(8,128)(2,1)} %collective-permute-done.1.refs_0_, bf16[96,1728]{1,0:T(8,128)(2,1)} %collective-permute-done.3.refs_1_, ...), custom_call_target="tpu_custom_call" | custom-call | flops 6000000000 | bytes 1 | tf_op jit(solution)/shard_map/pallas_call | solution.py:83
  88.8 12.2 %all-to-all-done.1.refs_1_.rt_ref = bf16[8,4,48,512]{3,2,1,0:T(8,128)(2,1)S(1)} async-done(((bf16[8,4,48,512]{3,2,1,0:T(8,128)(2,1)}), bf16[8,4,48,512]{3,2,1,0:T(8,128)(2,1)S(1)}, u32[]{:S(2)}, u32[]{:S(2)}) %all-to-all-start.1) | async-done | bytes 1572896 | tf_op jit(solution)/shard_map/all_to_all | solution.py:307
  101.0 1.2 copy-done.4
  102.2 24.0 %all_to_all.25.parts_ref = bf16[8,4,48,512]{3,2,1,0:T(8,128)(2,1)S(1)} all-to-all(bf16[8,4,48,512]{3,2,1,0:T(8,128)(2,1)} %shard_map.72), channel_id=1, replica_groups=mesh['zh'=2,'x'=4,'c'=2,'zl'=2,'y'=4] {'zl','y'}, dimensions={0} | all-to-all | bytes 3145728 | tf_op jit(solution)/shard_map/all_to_all | solution.py:308
  126.2 1.4 shard_map.73
  127.6 3.7 %all-to-all-start.3 = ((bf16[8,4,48,512]{3,2,1,0:T(8,128)(2,1)}), bf16[8,4,48,512]{3,2,1,0:T(8,128)(2,1)S(1)}, u32[]{:S(2)}, u32[]{:S(2)}) async-start(bf16[8,4,48,512]{3,2,1,0:T(8,128)(2,1)} %shard_map.73), calls=%async_computation.3 | async-start | bytes 3145728 | tf_op jit(solution)/shard_map/all_to_all | solution.py:309
  131.5 0.1 reshape.38.freqs_ref
  131.6 0.1 cosine_multiply_fusion.cosines_ref
  131.8 5.6 %shard_map.74 = (bf16[8,384,384]{2,1,0:T(8,128)(2,1)S(1)}, bf16[8,48,384]{2,1,0:T(8,128)(2,1)S(1)}) custom-call(s32[1]{0:T(128)} %bitcast.5.info, s32[8,48,1]{2,1,0:T(8,128)S(1)} %reshape.38.freqs_ref, f32[64,64]{1,0:T(8,128)S(1)} %cosine_multiply_fusion.cosines_ref), custom_call_target="tpu_custom_call" | custom-call | flops 1000000000 | bytes 4000000 | tf_op jit(solution)/shard_map/pallas_call | solution.py:255
  137.4 1.4 copy-done
  138.8 0.7 copy-done.1
  139.5 11.5 %shard_map.75 = (bf16[1728,3072]{1,0:T(8,128)(2,1)}, bf16[8,24,1728]{2,1,0:T(8,128)(2,1)}, bf16[8,24,1728]{2,1,0:T(8,128)(2,1)}) custom-call(s32[4]{0:T(128)} %get-tuple-element.17.info, bf16[1728,512]{1,0:T(8,128)(2,1)} %bitcast.31, bf16[8,4,48,512]{3,2,1,0:T(8,128)(2,1)} %copy-done.4, bf16[1728,3072]{1,0:T(8,128)(2,1)} %bitcast.26, ...), custom_call_target="tpu_custom_call" | custom-call | flops 4331667456 | bytes 12386304 | tf_op jit(solution)/shard_map/pallas_call | solution.py:203
  151.0 1.7 all-to-all-done.3.rt_ref
  152.6 1.2 copy-done.3
  153.8 9.7 %shard_map.77 = (bf16[8,24,1728]{2,1,0:T(8,128)(2,1)}, bf16[8,24,1728]{2,1,0:T(8,128)(2,1)}) custom-call(s32[4]{0:T(128)} %get-tuple-element.19.info, bf16[1728,512]{1,0:T(8,128)(2,1)} %bitcast.32, bf16[8,4,48,512]{3,2,1,0:T(8,128)(2,1)} %copy-done.3, bf16[1728,3072]{1,0:T(8,128)(2,1)} %bitcast.27, ...), custom_call_target="tpu_custom_call", output_to_operand_aliasing={{0}: (6, {}), {1}: (7, {})} | custom-call | flops 4331667456 | bytes 12386304 | tf_op jit(solution)/shard_map/pallas_call | solution.py:203
  163.6 0.9 collective-permute-start.23
  164.6 1.8 collective-permute-done.23
  166.4 2.1 %add_convert_fusion = bf16[8,24,1728]{2,1,0:T(8,128)(2,1)} fusion(bf16[8,24,1728]{2,1,0:T(8,128)(2,1)S(1)} %collective-permute-done.23, bf16[8,24,1728]{2,1,0:T(8,128)(2,1)} %get-tuple-element.14), kind=kLoop, calls=%fused_computation.1 | loop fusion | flops 1327104 | bytes 1990656 | tf_op jit(solution)/shard_map/convert_element_type | solution.py:316
  168.5 5.5 %all-to-all-start.4 = ((bf16[8,24,1728]{2,1,0:T(8,128)(2,1)}), bf16[8,24,1728]{2,1,0:T(8,128)(2,1)S(1)}, u32[]{:S(2)}, u32[]{:S(2)}) async-start(bf16[8,24,1728]{2,1,0:T(8,128)(2,1)} %add_convert_fusion), calls=%async_computation.4 | async-start | bytes 1376256 | tf_op jit(solution)/shard_map/all_to_all | solution.py:317
  174.0 0.3 convolution_multiply_fusion
  174.3 10.7 %shard_map.76 = bf16[1728,3072]{1,0:T(8,128)(2,1)} custom-call(s32[4]{0:T(128)} %get-tuple-element.19.info, bf16[1728,512]{1,0:T(8,128)(2,1)} %bitcast.33, bf16[8,4,48,512]{3,2,1,0:T(8,128)(2,1)} %copy-done.3, bf16[1728,3072]{1,0:T(8,128)(2,1)} %bitcast.28, bf16[8,384,384]{2,1,0:T(8,128)(2,1)} %copy-done, ...), custom_call_target="tpu_custom_call", output_to_operand_aliasing={{}: (6, {})} | custom-call | flops 4331667456 | bytes 12386304 | tf_op jit(solution)/shard_map/pallas_call | solution.py:203
  185.0 2.5 %all-to-all-done.4 = bf16[8,24,1728]{2,1,0:T(8,128)(2,1)S(1)} async-done(((bf16[8,24,1728]{2,1,0:T(8,128)(2,1)}), bf16[8,24,1728]{2,1,0:T(8,128)(2,1)S(1)}, u32[]{:S(2)}, u32[]{:S(2)}) %all-to-all-start.4) | async-done | bytes 663584 | tf_op jit(solution)/shard_map/all_to_all | solution.py:317
  187.5 0.1 convert_reduce_fusion
  187.6 2.3 %fusion = f32[3,64,1728]{2,1,0:T(8,128)} fusion(f32[3,8,64]{2,1,0:T(8,128)S(1)} %convolution_multiply_fusion, f32[24,1728]{1,0:T(8,128)S(1)} %convert_reduce_fusion), kind=kOutput, calls=%fused_computation.3 | convolution fusion | flops 31850496 | bytes 1499136 | tf_op jit(solution)/shard_map/ckf,ckj->cjf/dot_general | solution.py:323
  (59 shorter events, 0.6 us)
Async XLA Ops:
  0.6 19.9 %collective-permute-start.6 = (bf16[192,1728]{1,0:T(8,128)(2,1)}, bf16[192,1728]{1,0:T(8,128)(2,1)S(1)}, u32[]{:S(2)}, u32[]{:S(2)}) collective-permute-start(bf16[192,1728]{1,0:T(8,128)(2,1)} %bitcast.39), channel_id=1, source_target_pairs={{0,64},{1,65},{2,66},{3,67},{4,68},{5,69},{6,70},{7,71},{8,72},{9,... | collective-permute-start | bytes 1990664 | tf_op jit(solution)/shard_map/ppermute | solution.py:277
  5.1 16.6 %collective-permute-start = (bf16[192,1728]{1,0:T(8,128)(2,1)}, bf16[192,1728]{1,0:T(8,128)(2,1)S(1)}, u32[]{:S(2)}, u32[]{:S(2)}) collective-permute-start(bf16[192,1728]{1,0:T(8,128)(2,1)} %bitcast.40), channel_id=1, source_target_pairs={{0,48},{1,49},{2,50},{3,51},{4,52},{5,53},{6,54},{7,55},{8,56},{9,... | collective-permute-start | bytes 1990664 | tf_op jit(solution)/shard_map/ppermute | solution.py:277
  7.6 17.2 %collective-permute-start.2 = (bf16[192,1728]{1,0:T(8,128)(2,1)}, bf16[192,1728]{1,0:T(8,128)(2,1)}, u32[]{:S(2)}, u32[]{:S(2)}) collective-permute-start(bf16[192,1728]{1,0:T(8,128)(2,1)} %bitcast.41), channel_id=1, source_target_pairs={{0,16},{1,17},{2,18},{3,19},{4,20},{5,21},{6,22},{7,23},{8,24},{9,... | collective-permute-start | bytes 1990664 | tf_op jit(solution)/shard_map/ppermute | solution.py:277
  7.6 21.9 %collective-permute-start.19 = (bf16[192,1728]{1,0:T(8,128)(2,1)}, bf16[192,1728]{1,0:T(8,128)(2,1)}, u32[]{:S(2)}, u32[]{:S(2)}) collective-permute-start(bf16[192,1728]{1,0:T(8,128)(2,1)} %bitcast.42), channel_id=1, source_target_pairs={{0,8},{1,9},{2,10},{3,11},{4,12},{5,13},{6,14},{7,15},{8,0},{9,1},... | collective-permute-start | bytes 1990664 | tf_op jit(solution)/shard_map/ppermute | solution.py:277
  20.5 19.7 %copy-start.5 = (bf16[192,1728]{1,0:T(8,128)(2,1)}, bf16[192,1728]{1,0:T(8,128)(2,1)S(1)}, u32[]{:S(2)}) copy-start(bf16[192,1728]{1,0:T(8,128)(2,1)S(1)} %collective-permute-done.6.refs_2_) | copy-start | bytes 1990660
  20.5 17.1 %collective-permute-start.20 = (bf16[192,1728]{1,0:T(8,128)(2,1)S(1)}, bf16[192,1728]{1,0:T(8,128)(2,1)}, u32[]{:S(2)}, u32[]{:S(2)}) collective-permute-start(bf16[192,1728]{1,0:T(8,128)(2,1)S(1)} %collective-permute-done.6.refs_2_), channel_id=1, source_target_pairs={{0,8},{1,9},{2,10},{3,11},{4,12},{5,13},{6,14},{7,15},{8,0},{9,1},... | collective-permute-start | bytes 1990664 | tf_op jit(solution)/shard_map/ppermute | solution.py:277
  21.7 18.5 %copy-start.6 = (bf16[192,1728]{1,0:T(8,128)(2,1)}, bf16[192,1728]{1,0:T(8,128)(2,1)S(1)}, u32[]{:S(2)}) copy-start(bf16[192,1728]{1,0:T(8,128)(2,1)S(1)} %collective-permute-done.refs_4_) | copy-start | bytes 1990660
  21.7 16.6 %collective-permute-start.21 = (bf16[192,1728]{1,0:T(8,128)(2,1)S(1)}, bf16[192,1728]{1,0:T(8,128)(2,1)}, u32[]{:S(2)}, u32[]{:S(2)}) collective-permute-start(bf16[192,1728]{1,0:T(8,128)(2,1)S(1)} %collective-permute-done.refs_4_), channel_id=1, source_target_pairs={{0,8},{1,9},{2,10},{3,11},{4,12},{5,13},{6,14},{7,15},{8,0},{9,1},... | collective-permute-start | bytes 1990664 | tf_op jit(solution)/shard_map/ppermute | solution.py:277
  24.8 15.4 %collective-permute-start.22 = (bf16[192,1728]{1,0:T(8,128)(2,1)}, bf16[192,1728]{1,0:T(8,128)(2,1)}, u32[]{:S(2)}, u32[]{:S(2)}) collective-permute-start(bf16[192,1728]{1,0:T(8,128)(2,1)} %collective-permute-done.2.refs_6_), channel_id=1, source_target_pairs={{0,8},{1,9},{2,10},{3,11},{4,12},{5,13},{6,14},{7,15},{8,0},{9,1},... | collective-permute-start | bytes 1990664 | tf_op jit(solution)/shard_map/ppermute | solution.py:277
  27.0 9.9 %collective-permute-start.7 = (bf16[96,1728]{1,0:T(8,128)(2,1)S(1)}, bf16[96,1728]{1,0:T(8,128)(2,1)S(1)}, u32[]{:S(2)}, u32[]{:S(2)}) collective-permute-start(bf16[96,1728]{1,0:T(8,128)(2,1)S(1)} %get-tuple-element.21), channel_id=1, source_target_pairs={{0,48},{1,49},{2,50},{3,51},{4,52},{5,53},{6,54},{7,55},{8,56},{9,... | collective-permute-start | bytes 995336 | tf_op jit(solution)/shard_map/ppermute | solution.py:277
  29.5 23.1 %collective-permute-start.12 = (bf16[96,1728]{1,0:T(8,128)(2,1)S(1)}, bf16[96,1728]{1,0:T(8,128)(2,1)}, u32[]{:S(2)}, u32[]{:S(2)}) collective-permute-start(bf16[96,1728]{1,0:T(8,128)(2,1)S(1)} %get-tuple-element.20), channel_id=1, source_target_pairs={{0,16},{1,17},{2,18},{3,19},{4,20},{5,21},{6,22},{7,23},{8,24},{9,... | collective-permute-start | bytes 995336 | tf_op jit(solution)/shard_map/ppermute | solution.py:277
  36.9 21.4 %copy-start.8 = (bf16[96,1728]{1,0:T(8,128)(2,1)}, bf16[96,1728]{1,0:T(8,128)(2,1)S(1)}, u32[]{:S(2)}) copy-start(bf16[96,1728]{1,0:T(8,128)(2,1)S(1)} %collective-permute-done.7.refs_4_) | copy-start | bytes 995332
  36.9 18.4 %collective-permute-start.8 = (bf16[96,1728]{1,0:T(8,128)(2,1)S(1)}, bf16[96,1728]{1,0:T(8,128)(2,1)}, u32[]{:S(2)}, u32[]{:S(2)}) collective-permute-start(bf16[96,1728]{1,0:T(8,128)(2,1)S(1)} %get-tuple-element.20), channel_id=1, source_target_pairs={{0,48},{1,49},{2,50},{3,51},{4,52},{5,53},{6,54},{7,55},{8,56},{9,... | collective-permute-start | bytes 995336 | tf_op jit(solution)/shard_map/ppermute | solution.py:277
  37.6 17.7 %collective-permute-start.11 = (bf16[96,1728]{1,0:T(8,128)(2,1)S(1)}, bf16[96,1728]{1,0:T(8,128)(2,1)}, u32[]{:S(2)}, u32[]{:S(2)}) collective-permute-start(bf16[96,1728]{1,0:T(8,128)(2,1)S(1)} %get-tuple-element.21), channel_id=1, source_target_pairs={{0,16},{1,17},{2,18},{3,19},{4,20},{5,21},{6,22},{7,23},{8,24},{9,... | collective-permute-start | bytes 995336 | tf_op jit(solution)/shard_map/ppermute | solution.py:277
  38.4 19.9 %collective-permute-start.1 = (bf16[96,1728]{1,0:T(8,128)(2,1)S(1)}, bf16[96,1728]{1,0:T(8,128)(2,1)}, u32[]{:S(2)}, u32[]{:S(2)}) collective-permute-start(bf16[96,1728]{1,0:T(8,128)(2,1)S(1)} %slice.16), channel_id=1, source_target_pairs={{0,48},{1,49},{2,50},{3,51},{4,52},{5,53},{6,54},{7,55},{8,56},{9,... | collective-permute-start | bytes 995336 | tf_op jit(solution)/shard_map/ppermute | solution.py:277
  40.3 18.2 %collective-permute-start.3 = (bf16[96,1728]{1,0:T(8,128)(2,1)S(1)}, bf16[96,1728]{1,0:T(8,128)(2,1)}, u32[]{:S(2)}, u32[]{:S(2)}) collective-permute-start(bf16[96,1728]{1,0:T(8,128)(2,1)S(1)} %slice.17), channel_id=1, source_target_pairs={{0,16},{1,17},{2,18},{3,19},{4,20},{5,21},{6,22},{7,23},{8,24},{9,... | collective-permute-start | bytes 995336 | tf_op jit(solution)/shard_map/ppermute | solution.py:277
  48.1 25.9 %all-to-all-start = ((bf16[8,4,48,512]{3,2,1,0:T(8,128)(2,1)}), bf16[8,4,48,512]{3,2,1,0:T(8,128)(2,1)S(1)}, u32[]{:S(2)}, u32[]{:S(2)}) async-start(bf16[8,4,48,512]{3,2,1,0:T(8,128)(2,1)} %shard_map.69), calls=%async_computation | async-start | bytes 3145728 | tf_op jit(solution)/shard_map/all_to_all | solution.py:306
  52.6 7.4 %collective-permute-start.15 = (bf16[96,1728]{1,0:T(8,128)(2,1)S(1)}, bf16[96,1728]{1,0:T(8,128)(2,1)S(1)}, u32[]{:S(2)}, u32[]{:S(2)}) collective-permute-start(bf16[96,1728]{1,0:T(8,128)(2,1)S(1)} %collective-permute-done.7.refs_4_), channel_id=1, source_target_pairs={{0,48},{1,49},{2,50},{3,51},{4,52},{5,53},{6,54},{7,55},{8,56},{9,... | collective-permute-start | bytes 995336 | tf_op jit(solution)/shard_map/ppermute | solution.py:277
  55.3 8.3 %collective-permute-start.16 = (bf16[96,1728]{1,0:T(8,128)(2,1)}, bf16[96,1728]{1,0:T(8,128)(2,1)S(1)}, u32[]{:S(2)}, u32[]{:S(2)}) collective-permute-start(bf16[96,1728]{1,0:T(8,128)(2,1)} %collective-permute-done.12.refs_9_), channel_id=1, source_target_pairs={{0,16},{1,17},{2,18},{3,19},{4,20},{5,21},{6,22},{7,23},{8,24},{9,... | collective-permute-start | bytes 995336 | tf_op jit(solution)/shard_map/ppermute | solution.py:277
  55.3 11.9 %collective-permute-start.14 = (bf16[96,1728]{1,0:T(8,128)(2,1)}, bf16[96,1728]{1,0:T(8,128)(2,1)S(1)}, u32[]{:S(2)}, u32[]{:S(2)}) collective-permute-start(bf16[96,1728]{1,0:T(8,128)(2,1)} %collective-permute-done.12.refs_9_), channel_id=1, source_target_pairs={{0,8},{1,9},{2,10},{3,11},{4,12},{5,13},{6,14},{7,15},{8,0},{9,1},... | collective-permute-start | bytes 995336 | tf_op jit(solution)/shard_map/ppermute | solution.py:277
  58.3 9.0 %collective-permute-start.9 = (bf16[96,1728]{1,0:T(8,128)(2,1)S(1)}, bf16[96,1728]{1,0:T(8,128)(2,1)S(1)}, u32[]{:S(2)}, u32[]{:S(2)}) collective-permute-start(bf16[96,1728]{1,0:T(8,128)(2,1)S(1)} %collective-permute-done.7.refs_4_), channel_id=1, source_target_pairs={{0,8},{1,9},{2,10},{3,11},{4,12},{5,13},{6,14},{7,15},{8,0},{9,1},... | collective-permute-start | bytes 995336 | tf_op jit(solution)/shard_map/ppermute | solution.py:277
  58.4 9.4 %collective-permute-start.10 = (bf16[96,1728]{1,0:T(8,128)(2,1)}, bf16[96,1728]{1,0:T(8,128)(2,1)S(1)}, u32[]{:S(2)}, u32[]{:S(2)}) collective-permute-start(bf16[96,1728]{1,0:T(8,128)(2,1)} %collective-permute-done.8.refs_5_), channel_id=1, source_target_pairs={{0,8},{1,9},{2,10},{3,11},{4,12},{5,13},{6,14},{7,15},{8,0},{9,1},... | collective-permute-start | bytes 995336 | tf_op jit(solution)/shard_map/ppermute | solution.py:277
  60.0 7.3 %copy-start.9 = (bf16[96,1728]{1,0:T(8,128)(2,1)}, bf16[96,1728]{1,0:T(8,128)(2,1)S(1)}, u32[]{:S(2)}) copy-start(bf16[96,1728]{1,0:T(8,128)(2,1)S(1)} %collective-permute-done.15.refs_12_) | copy-start | bytes 995332
  60.0 7.9 %collective-permute-start.13 = (bf16[96,1728]{1,0:T(8,128)(2,1)}, bf16[96,1728]{1,0:T(8,128)(2,1)S(1)}, u32[]{:S(2)}, u32[]{:S(2)}) collective-permute-start(bf16[96,1728]{1,0:T(8,128)(2,1)} %collective-permute-done.11.refs_8_), channel_id=1, source_target_pairs={{0,8},{1,9},{2,10},{3,11},{4,12},{5,13},{6,14},{7,15},{8,0},{9,1},... | collective-permute-start | bytes 995336 | tf_op jit(solution)/shard_map/ppermute | solution.py:277
  63.6 7.7 %copy-start.10 = (bf16[96,1728]{1,0:T(8,128)(2,1)}, bf16[96,1728]{1,0:T(8,128)(2,1)S(1)}, u32[]{:S(2)}) copy-start(bf16[96,1728]{1,0:T(8,128)(2,1)S(1)} %collective-permute-done.16.refs_13_) | copy-start | bytes 995332
  63.6 5.1 %collective-permute-start.4 = (bf16[96,1728]{1,0:T(8,128)(2,1)}, bf16[96,1728]{1,0:T(8,128)(2,1)S(1)}, u32[]{:S(2)}, u32[]{:S(2)}) collective-permute-start(bf16[96,1728]{1,0:T(8,128)(2,1)} %collective-permute-done.1.refs_0_), channel_id=1, source_target_pairs={{0,8},{1,9},{2,10},{3,11},{4,12},{5,13},{6,14},{7,15},{8,0},{9,1},... | collective-permute-start | bytes 995336 | tf_op jit(solution)/shard_map/ppermute | solution.py:277
  67.2 2.9 %copy-start.11 = (bf16[96,1728]{1,0:T(8,128)(2,1)}, bf16[96,1728]{1,0:T(8,128)(2,1)S(1)}, u32[]{:S(2)}) copy-start(bf16[96,1728]{1,0:T(8,128)(2,1)S(1)} %collective-permute-done.14.refs_11_.refs_5_) | copy-start | bytes 995332
  67.2 2.0 %collective-permute-start.5 = (bf16[96,1728]{1,0:T(8,128)(2,1)}, bf16[96,1728]{1,0:T(8,128)(2,1)S(1)}, u32[]{:S(2)}, u32[]{:S(2)}) collective-permute-start(bf16[96,1728]{1,0:T(8,128)(2,1)} %collective-permute-done.3.refs_1_), channel_id=1, source_target_pairs={{0,8},{1,9},{2,10},{3,11},{4,12},{5,13},{6,14},{7,15},{8,0},{9,1},... | collective-permute-start | bytes 995336 | tf_op jit(solution)/shard_map/ppermute | solution.py:277
  67.3 2.8 %copy-start.12 = (bf16[96,1728]{1,0:T(8,128)(2,1)}, bf16[96,1728]{1,0:T(8,128)(2,1)S(1)}, u32[]{:S(2)}) copy-start(bf16[96,1728]{1,0:T(8,128)(2,1)S(1)} %collective-permute-done.9.refs_6_.refs_2_) | copy-start | bytes 995332
  67.3 2.6 %collective-permute-start.17 = (bf16[96,1728]{1,0:T(8,128)(2,1)S(1)}, bf16[96,1728]{1,0:T(8,128)(2,1)S(1)}, u32[]{:S(2)}, u32[]{:S(2)}) collective-permute-start(bf16[96,1728]{1,0:T(8,128)(2,1)S(1)} %collective-permute-done.15.refs_12_), channel_id=1, source_target_pairs={{0,8},{1,9},{2,10},{3,11},{4,12},{5,13},{6,14},{7,15},{8,0},{9,1},... | collective-permute-start | bytes 995336 | tf_op jit(solution)/shard_map/ppermute | solution.py:277
  67.8 2.3 %copy-start.13 = (bf16[96,1728]{1,0:T(8,128)(2,1)}, bf16[96,1728]{1,0:T(8,128)(2,1)S(1)}, u32[]{:S(2)}) copy-start(bf16[96,1728]{1,0:T(8,128)(2,1)S(1)} %collective-permute-done.10.refs_7_.refs_3_) | copy-start | bytes 995332
  67.8 2.3 %collective-permute-start.18 = (bf16[96,1728]{1,0:T(8,128)(2,1)S(1)}, bf16[96,1728]{1,0:T(8,128)(2,1)}, u32[]{:S(2)}, u32[]{:S(2)}) collective-permute-start(bf16[96,1728]{1,0:T(8,128)(2,1)S(1)} %collective-permute-done.16.refs_13_), channel_id=1, source_target_pairs={{0,8},{1,9},{2,10},{3,11},{4,12},{5,13},{6,14},{7,15},{8,0},{9,1},... | collective-permute-start | bytes 995336 | tf_op jit(solution)/shard_map/ppermute | solution.py:277
  67.9 2.0 %copy-start.14 = (bf16[96,1728]{1,0:T(8,128)(2,1)}, bf16[96,1728]{1,0:T(8,128)(2,1)S(1)}, u32[]{:S(2)}) copy-start(bf16[96,1728]{1,0:T(8,128)(2,1)S(1)} %collective-permute-done.13.refs_10_.refs_4_) | copy-start | bytes 995332
  68.7 1.3 copy-start.15
  69.2 0.8 copy-start.16
  70.0 0.8 copy-start.17
  74.0 0.7 copy-start.2
  76.0 25.0 %all-to-all-start.1 = ((bf16[8,4,48,512]{3,2,1,0:T(8,128)(2,1)}), bf16[8,4,48,512]{3,2,1,0:T(8,128)(2,1)S(1)}, u32[]{:S(2)}, u32[]{:S(2)}) async-start(bf16[8,4,48,512]{3,2,1,0:T(8,128)(2,1)} %shard_map.71), calls=%async_computation.1 | async-start | bytes 3145728 | tf_op jit(solution)/shard_map/all_to_all | solution.py:307
  101.0 1.2 copy-start.4
  127.6 3.7 %copy-start.7 = (s32[48,8]{0,1:T(8,128)S(1)}, s32[48,8]{0,1:T(8,128)}, u32[]{:S(2)}) copy-start(s32[48,8]{0,1:T(8,128)} %param.9) | copy-start | bytes 4612
  127.6 25.1 %all-to-all-start.3 = ((bf16[8,4,48,512]{3,2,1,0:T(8,128)(2,1)}), bf16[8,4,48,512]{3,2,1,0:T(8,128)(2,1)S(1)}, u32[]{:S(2)}, u32[]{:S(2)}) async-start(bf16[8,4,48,512]{3,2,1,0:T(8,128)(2,1)} %shard_map.73), calls=%async_computation.3 | async-start | bytes 3145728 | tf_op jit(solution)/shard_map/all_to_all | solution.py:309
  137.4 1.4 copy-start
  138.8 0.7 copy-start.1
  152.6 1.2 copy-start.3
  163.6 2.8 %collective-permute-start.23 = (bf16[8,24,1728]{2,1,0:T(8,128)(2,1)}, bf16[8,24,1728]{2,1,0:T(8,128)(2,1)S(1)}, u32[]{:S(2)}, u32[]{:S(2)}) collective-permute-start(bf16[8,24,1728]{2,1,0:T(8,128)(2,1)} %get-tuple-element.15), channel_id=1, source_target_pairs={{0,8},{1,9},{2,10},{3,11},{4,12},{5,13},{6,14},{7,15},{8,0},{9,1},... | collective-permute-start | bytes 1990664 | tf_op jit(solution)/shard_map/ppermute | solution.py:277
  168.5 19.0 %all-to-all-start.4 = ((bf16[8,24,1728]{2,1,0:T(8,128)(2,1)}), bf16[8,24,1728]{2,1,0:T(8,128)(2,1)S(1)}, u32[]{:S(2)}, u32[]{:S(2)}) async-start(bf16[8,24,1728]{2,1,0:T(8,128)(2,1)} %add_convert_fusion), calls=%async_computation.4 | async-start | bytes 1376256 | tf_op jit(solution)/shard_map/all_to_all | solution.py:317
